TPU v7x, 512 devices: a whole 4x8x8 slice. The times are simulated.
512 devices in a mesh: seq: 128 (over y, z, core), head: 4 (over x).
Axes of the slice: x: 4, y: 8, z: 8, core: 2. Of those that a mesh axis runs over, the one named last changes fastest.
Arguments:
- queries: bfloat16 [32768, 4096], P(('seq', 'head')), may hold values from -1 to 1
- keys: bfloat16 [32768, 1024], P(('seq', 'head')), may hold values from -2.5 to 2.5
- values: bfloat16 [32768, 1024], P(('seq', 'head')), may hold values from -3 to 3
- outputs_saved: bfloat16 [32768, 4096], P(('seq', 'head')), may hold values from -3 to 3
- grad_out: bfloat16 [32768, 4096], P(('seq', 'head')), may hold values from -3 to 3
- lse: float32 [32768, 32], P('seq', 'head'), may hold values from 2.5 to 4
- block_lists: int32 [256, 32, 4], P(None, 'head'), may hold values from 0 to 511, as said below
Outputs:
- grad_queries: bfloat16 [32768, 4096], P(('seq', 'head'))
- grad_keys: bfloat16 [32768, 1024], P(('seq', 'head'))
- grad_values: bfloat16 [32768, 1024], P(('seq', 'head'))
Inputs may be any that keep to these rules, and one draw needn't show every extreme that they name: `block_lists`: key block j lies in sequence shard j // 4. No query block lists a key block of its own sequence shard. For the query blocks of one sequence shard and the 8 query heads held by one device along `head`, at most 1 listed block lies in any one other sequence shard; a few shards are listed far more often than the others.
All inputs are finite; a program needn't handle non-finite values.
Results may differ from a plain program's by a relative error of at most 0.011.
Values may be sent and summed in bfloat16 or wider, within the bound.
A program may use at most 128 MiB of HBM per device.

v0:
```python
import math

import jax
import jax.numpy as jnp
from jax import lax
from jax.sharding import PartitionSpec as P

HD = 128
QB = 128
KB = 64
NSEL = 4
GROUP = 4


def remote_terms(q_rows, o_grad, lse_rows, delta_rows, k_rows, v_rows):
    scaling = HD ** (-0.5)
    logit_scores = (
        jnp.einsum("nkd,nqd->nkq", k_rows, q_rows, preferred_element_type=jnp.float32) * scaling
    )
    probability = jnp.exp(logit_scores - lse_rows[:, None, :])
    grad_prob = jnp.einsum("nkd,nqd->nkq", v_rows, o_grad, preferred_element_type=jnp.float32)
    score_gradient = probability * (grad_prob - delta_rows[:, None, :])
    prob_low = probability.astype(jnp.bfloat16)
    score_low = score_gradient.astype(jnp.bfloat16)
    dq_part = (
        jnp.einsum("nkq,nkd->nqd", score_low, k_rows, preferred_element_type=jnp.float32) * scaling
    )
    dk_part = (
        jnp.einsum("nkq,nqd->nkd", score_low, q_rows, preferred_element_type=jnp.float32) * scaling
    )
    dv_part = jnp.einsum("nkq,nqd->nkd", prob_low, o_grad, preferred_element_type=jnp.float32)
    return (
        dq_part.astype(jnp.bfloat16),
        dk_part.astype(jnp.bfloat16),
        dv_part.astype(jnp.bfloat16),
    )


def in_groups(handler, arrays, slot_count):
    group_size = math.gcd(slot_count, 16)
    shaped = tuple(
        (
            entry.reshape((slot_count // group_size, group_size) + entry.shape[1:])
            for entry in arrays
        )
    )
    results = lax.map(lambda fragments: handler(*fragments), shaped)
    return tuple((entry.reshape((slot_count,) + entry.shape[2:]) for entry in results))


def own_terms(q_five, do_five, k_four, v_four, lse_four, delta_four):
    scaling = HD ** (-0.5)
    block_rows = q_five.shape[1]
    causal = lax.broadcasted_iota(jnp.int32, (block_rows, block_rows), 0) <= lax.broadcasted_iota(
        jnp.int32, (block_rows, block_rows), 1
    )
    logit_scores = (
        jnp.einsum("bshd,bqhgd->bhgsq", k_four, q_five, preferred_element_type=jnp.float32)
        * scaling
    )
    probability = jnp.where(
        causal, jnp.exp(logit_scores - lse_four[:, :, :, None, :]), jnp.float32(0.0)
    )
    grad_prob = jnp.einsum("bshd,bqhgd->bhgsq", v_four, do_five, preferred_element_type=jnp.float32)
    score_gradient = probability * (grad_prob - delta_four[:, :, :, None, :])
    prob_low = probability.astype(jnp.bfloat16)
    score_low = score_gradient.astype(jnp.bfloat16)
    dq_own = (
        jnp.einsum("bhgsq,bshd->bqhgd", score_low, k_four, preferred_element_type=jnp.float32)
        * scaling
    )
    dk_own = (
        jnp.einsum("bhgsq,bqhgd->bshd", score_low, q_five, preferred_element_type=jnp.float32)
        * scaling
    )
    dv_own = jnp.einsum("bhgsq,bqhgd->bshd", prob_low, do_five, preferred_element_type=jnp.float32)
    return (dq_own, dk_own, dv_own)


def body(queries, keys, values, outputs_saved, grad_out, lse, block_lists):
    heads_here = lse.shape[1]
    q_head, do_head, o_head, k_head, v_head = (
        lax.all_to_all(queries, "head", split_axis=1, concat_axis=0, tiled=True),
        lax.all_to_all(grad_out, "head", split_axis=1, concat_axis=0, tiled=True),
        lax.all_to_all(outputs_saved, "head", split_axis=1, concat_axis=0, tiled=True),
        lax.all_to_all(keys, "head", split_axis=1, concat_axis=0, tiled=True),
        lax.all_to_all(values, "head", split_axis=1, concat_axis=0, tiled=True),
    )
    products = do_head.astype(jnp.float32) * o_head.astype(jnp.float32)
    delta_head = jnp.sum(products.reshape(q_head.shape[0], heads_here, HD), axis=-1)
    token_count = q_head.shape[0]
    kv_here = k_head.shape[1] // HD
    blocks_here = token_count // QB
    key_count = token_count // KB
    q_five = q_head.reshape(blocks_here, QB, kv_here, GROUP, HD)
    do_five = do_head.reshape(blocks_here, QB, kv_here, GROUP, HD)
    k_four = k_head.reshape(blocks_here, QB, kv_here, HD)
    v_four = v_head.reshape(blocks_here, QB, kv_here, HD)
    lse_four = lse.reshape(blocks_here, QB, kv_here, GROUP).transpose(0, 2, 3, 1)
    delta_four = delta_head.reshape(blocks_here, QB, kv_here, GROUP).transpose(0, 2, 3, 1)
    dq_own, dk_own, dv_own = own_terms(q_five, do_five, k_four, v_four, lse_four, delta_four)
    neighbour_count = lax.axis_size("seq")
    seq_here = lax.axis_index("seq")
    per_peer = block_lists.reshape(neighbour_count, -1)
    request_count = per_peer.shape[1]
    capacity = (request_count + neighbour_count - 2) // (neighbour_count - 1)
    slot_count = neighbour_count * capacity
    owner_of = per_peer // key_count
    order_ids = jnp.arange(request_count, dtype=jnp.int32)
    earlier = (owner_of[:, :, None] == owner_of[:, None, :]) & (
        order_ids[None, :] < order_ids[:, None]
    )[None, :, :]
    position = jnp.sum(earlier.astype(jnp.int32), axis=2)
    mine_owner = lax.dynamic_index_in_dim(owner_of, seq_here, 0, keepdims=False)
    mine_position = lax.dynamic_index_in_dim(position, seq_here, 0, keepdims=False)
    slots = mine_owner * capacity + mine_position
    hits = (
        (owner_of == seq_here)[:, :, None]
        & (position[:, :, None] == jnp.arange(capacity, dtype=jnp.int32)[None, None, :])
    ).astype(jnp.int32)
    slot_used = jnp.sum(hits, axis=1).reshape(-1)
    local_block = jnp.sum(hits * (per_peer % key_count)[:, :, None], axis=1).reshape(-1)
    head_of_request = order_ids % (heads_here * NSEL) // NSEL
    kv_slot = jnp.sum(hits * (head_of_request // GROUP)[None, :, None], axis=1).reshape(-1)
    unit_index = local_block * kv_here + kv_slot
    selector = (
        (jnp.arange(key_count * kv_here, dtype=jnp.int32)[:, None] == unit_index[None, :])
        & (slot_used[None, :] > 0)
    ).astype(jnp.bfloat16)
    q_pairs = (
        q_head.reshape(blocks_here, QB, heads_here, HD).transpose(0, 2, 1, 3).reshape(-1, QB, HD)
    )
    do_pairs = (
        do_head.reshape(blocks_here, QB, heads_here, HD).transpose(0, 2, 1, 3).reshape(-1, QB, HD)
    )
    lse_pairs = lse.reshape(blocks_here, QB, heads_here).transpose(0, 2, 1).reshape(-1, QB)
    delta_pairs = delta_head.reshape(blocks_here, QB, heads_here).transpose(0, 2, 1).reshape(-1, QB)
    pair_index = order_ids // NSEL
    key_blocks = k_head.reshape(key_count, KB, kv_here, HD)
    value_blocks = v_head.reshape(key_count, KB, kv_here, HD)
    send_rows = jnp.concatenate([q_pairs, do_pairs], axis=-1)[pair_index]
    send_stats = jnp.stack([lse_pairs, delta_pairs], axis=1)[pair_index]
    row_buffer = jnp.zeros((slot_count, QB, 2 * HD), jnp.bfloat16).at[slots].set(send_rows)
    stat_buffer = jnp.zeros((slot_count, 2, QB), jnp.float32).at[slots].set(send_stats)
    arrived = lax.all_to_all(row_buffer, "seq", split_axis=0, concat_axis=0, tiled=True)
    arrived_stats = lax.all_to_all(stat_buffer, "seq", split_axis=0, concat_axis=0, tiled=True)
    k_rows = key_blocks[local_block, :, kv_slot]
    v_rows = value_blocks[local_block, :, kv_slot]
    dq_slots, dk_slots, dv_slots = in_groups(
        remote_terms,
        (
            arrived[..., :HD],
            arrived[..., HD:],
            arrived_stats[:, 0],
            arrived_stats[:, 1],
            k_rows,
            v_rows,
        ),
        slot_count,
    )
    returned = lax.all_to_all(dq_slots, "seq", split_axis=0, concat_axis=0, tiled=True)
    dq_requests = returned[slots]
    dkv_parts = jnp.concatenate([dk_slots, dv_slots], axis=-1)
    unit_sums = jnp.dot(
        selector, dkv_parts.reshape(slot_count, -1), preferred_element_type=jnp.float32
    )
    unit_sums = unit_sums.reshape(key_count, kv_here, KB, 2 * HD).transpose(0, 2, 1, 3)
    listed_k = unit_sums[..., :HD].reshape(token_count, kv_here * HD)
    listed_v = unit_sums[..., HD:].reshape(token_count, kv_here * HD)
    grad_k = (dk_own.reshape(token_count, kv_here * HD) + listed_k).astype(jnp.bfloat16)
    grad_v = (dv_own.reshape(token_count, kv_here * HD) + listed_v).astype(jnp.bfloat16)
    dq_listed = (
        dq_requests.astype(jnp.float32)
        .reshape(blocks_here, heads_here, NSEL, QB, HD)
        .sum(axis=2)
        .transpose(0, 2, 1, 3)
    )
    grad_q = (
        (dq_own.reshape(blocks_here, QB, heads_here, HD) + dq_listed)
        .astype(jnp.bfloat16)
        .reshape(token_count, heads_here * HD)
    )
    grad_queries, grad_keys, grad_values = (
        lax.all_to_all(grad_q, "head", split_axis=0, concat_axis=1, tiled=True),
        lax.all_to_all(grad_k, "head", split_axis=0, concat_axis=1, tiled=True),
        lax.all_to_all(grad_v, "head", split_axis=0, concat_axis=1, tiled=True),
    )
    return (grad_queries, grad_keys, grad_values)


def solution(mesh):
    in_specs = (
        P(("seq", "head"), None),
        P(("seq", "head"), None),
        P(("seq", "head"), None),
        P(("seq", "head"), None),
        P(("seq", "head"), None),
        P("seq", "head"),
        P(None, "head", None),
    )
    out_specs = (P(("seq", "head"), None), P(("seq", "head"), None), P(("seq", "head"), None))
    return jax.shard_map(body, mesh=mesh, in_specs=in_specs, out_specs=out_specs, check_vma=False)
```

profile of v0, /device:TPU:96, one launch (start us, length us, event | category | flops | bytes accessed | tf_op | source)
XLA Modules:
  0.0 570.5 jit_solution(11842360470757217295)
XLA Ops:
  0.7 1.9 copy.277
  2.6 4.4 all-to-all-start.2
  7.0 1.9 copy.276
  8.9 7.6 %all-to-all-done.2 = bf16[64,4,1024]{2,0,1:T(8,128)(2,1)S(1)} async-done(((bf16[64,4,1024]{2,0,1:T(8,128)(2,1)}), bf16[64,4,1024]{2,0,1:T(8,128)(2,1)S(1)}, u32[]{:S(2)}, u32[]{:S(2)}) %all-to-all-start.2) | async-done | bytes 524320 | tf_op jit(solution)/shard_map/all_to_all | solution.py:84
  16.5 3.5 all-to-all-start.4
  22.8 5.4 all-to-all-done.4
  28.2 3.5 all-to-all-start
  35.2 4.6 all-to-all-done
  39.8 3.3 all-to-all-start.1
  43.1 1.9 bitcast_bitcast_fusion
  47.0 1.6 reduce_sum.72
  49.0 4.4 all-to-all-start.3
  55.5 6.9 %scatter_fusion.1 = f32[128,2,128]{2,1,0:T(2,128)} fusion(f32[128,2,128]{2,1,0:T(2,128)} %broadcast_in_dim.27, s32[64]{0:T(128)S(1)} %get-tuple-element.93, f32[64,2,128]{2,1,0:T(2,128)S(1)} %gather_fusion.2), kind=kCustom, calls=%fused_computation.6 | custom fusion | bytes 196864 | tf_op jit(solution)/shard_map/scatter | solution.py:144
  62.4 16.4 %all-to-all-start.6 = ((f32[128,2,128]{2,1,0:T(2,128)}), f32[128,2,128]{2,1,0:T(2,128)S(1)}, u32[]{:S(2)}, u32[]{:S(2)}) async-start(f32[128,2,128]{2,1,0:T(2,128)} %scatter_fusion.1), calls=%async_computation.6 | async-start | bytes 262144 | tf_op jit(solution)/shard_map/all_to_all | solution.py:146
  81.3 2.8 gather_fusion.1
  84.1 4.3 broadcast_in_dim.26
  88.3 11.9 %scatter_fusion = bf16[128,128,256]{2,1,0:T(8,128)(2,1)} fusion(bf16[128,128,256]{2,1,0:T(8,128)(2,1)} %broadcast_in_dim.26, s32[64]{0:T(128)S(1)} %get-tuple-element.93, bf16[64,128,256]{2,1,0:T(8,128)(2,1)} %gather_fusion.1), kind=kCustom, calls=%fused_computation.5 | custom fusion | bytes 12583168 | tf_op jit(solution)/shard_map/scatter | solution.py:143
  100.9 14.2 %all-to-all-start.5 = ((bf16[128,128,256]{2,1,0:T(8,128)(2,1)}), bf16[128,128,256]{2,1,0:T(8,128)(2,1)}, u32[]{:S(2)}, u32[]{:S(2)}) async-start(bf16[128,128,256]{2,1,0:T(8,128)(2,1)} %scatter_fusion), calls=%async_computation.5 | async-start | bytes 16777216 | tf_op jit(solution)/shard_map/all_to_all | solution.py:145
  117.2 9.1 %convert_reduce_fusion.2 = (s32[256]{0:T(256)S(1)}, s32[256]{0:T(256)S(1)}) fusion(pred[256,8,4]{2,1,0:T(8,128)(4,1)S(1)} %copy.187, s32[256,8,4]{2,1,0:T(8,128)S(1)} %copy.182, pred[256,8,4]{2,1,0:T(8,128)(4,1)S(1)} %eq.90, s32[]{:T(128)S(6)} %axis_index.15), kind=kLoop, calls=%fused_computation.78 | loop fusion | flops 196096 | bytes 51204 | tf_op jit(solution)/shard_map/reduce_sum | solution.py:121
  128.3 2.3 gather_fusion.3
  131.7 220.3 %all-to-all-done.5 = bf16[128,128,256]{2,1,0:T(8,128)(2,1)} async-done(((bf16[128,128,256]{2,1,0:T(8,128)(2,1)}), bf16[128,128,256]{2,1,0:T(8,128)(2,1)}, u32[]{:S(2)}, u32[]{:S(2)}) %all-to-all-start.5) | async-done | bytes 8388640 | tf_op jit(solution)/shard_map/all_to_all | solution.py:145
  352.0 6.0 %fusion.80 = (bf16[128,128,128]{2,1,0:T(8,128)(2,1)}, bf16[128,128,128]{2,1,0:T(8,128)(2,1)}) fusion(bf16[128,128,256]{2,1,0:T(8,128)(2,1)} %all-to-all-done.5), kind=kLoop, calls=%fused_computation.161 | loop fusion | bytes 16777216 | tf_op jit(solution)/shard_map/slice | solution.py:153
  358.0 66.5 %while.14 = (s32[]{:T(128)}, bf16[8,16,128,128]{3,2,1,0:T(8,128)(2,1)}, bf16[8,16,64,128]{3,2,1,0:T(8,128)(2,1)}, bf16[8,16,64,128]{3,2,1,0:T(8,128)(2,1)}, bf16...) while((s32[]{:T(128)}, ...), condition=%wide.region_8.9_spmd, body=%wide.region_7.8_spmd.sunk | while | flops 169476096 | bytes 6345841 | solution.py:47
  358.0 1.5 fusion.114
  359.6 1.6 fusion.115
  362.3 2.0 fusion.117
  364.4 2.0 fusion.118
  367.9 1.6 fusion.115
  370.6 2.0 fusion.117
  372.7 2.0 fusion.118
  376.2 1.6 fusion.115
  379.0 2.0 fusion.117
  381.0 2.0 fusion.118
  384.5 1.6 fusion.115
  387.3 2.0 fusion.117
  389.3 2.0 fusion.118
  392.8 1.6 fusion.115
  395.6 2.0 fusion.117
  397.6 2.0 fusion.118
  401.1 1.6 fusion.115
  403.9 2.0 fusion.117
  405.9 2.0 fusion.118
  407.9 1.5 fusion.114
  409.4 1.6 fusion.115
  412.2 2.1 fusion.117
  414.2 2.0 fusion.118
  416.3 1.5 fusion.114
  417.8 1.6 fusion.115
  420.5 2.0 fusion.117
  422.5 2.0 fusion.118
  424.6 10.4 %all-to-all-start.7 = ((bf16[128,128,128]{2,1,0:T(8,128)(2,1)}), bf16[128,128,128]{2,1,0:T(8,128)(2,1)}, u32[]{:S(2)}, u32[]{:S(2)}) async-start(bf16[128,128,128]{2,1,0:T(8,128)(2,1)} %bitcast.247), calls=%async_computation.7 | async-start | bytes 8388608 | tf_op jit(solution)/shard_map/all_to_all | solution.py:161
  441.4 1.5 fusion.45
  443.3 2.2 convolution_multiply_fusion.3
  445.5 4.4 pad_maximum_fusion
  449.9 6.9 %copy.210 = bf16[128,64,256]{0,2,1:T(8,128)(2,1)} copy(bf16[128,64,256]{2,1,0:T(8,128)(2,1)} %pad_maximum_fusion) | data formatting | bytes 8388608 | tf_op jit(solution)/shard_map/concatenate | solution.py:163
  456.8 3.4 fusion.41
  462.6 75.4 %all-to-all-done.7 = bf16[128,128,128]{2,1,0:T(8,128)(2,1)} async-done(((bf16[128,128,128]{2,1,0:T(8,128)(2,1)}), bf16[128,128,128]{2,1,0:T(8,128)(2,1)}, u32[]{:S(2)}, u32[]{:S(2)}) %all-to-all-start.7) | async-done | bytes 4194336 | tf_op jit(solution)/shard_map/all_to_all | solution.py:161
  538.0 4.9 all-to-all-start.10
  542.9 3.1 gather_fusion.4
  546.4 2.5 all-to-all-done.10
  548.8 3.3 all-to-all-start.9
  554.9 3.2 all-to-all-done.9
  558.1 3.5 all-to-all-start.8
  562.9 6.7 %all-to-all-done.8 = bf16[4,64,1024]{2,1,0:T(8,128)(2,1)S(1)} async-done(((bf16[4,64,1024]{2,1,0:T(8,128)(2,1)}), bf16[4,64,1024]{2,1,0:T(8,128)(2,1)S(1)}, u32[]{:S(2)}, u32[]{:S(2)}) %all-to-all-start.8) | async-done | bytes 524320 | tf_op jit(solution)/shard_map/all_to_all | solution.py:184
  (142 shorter events, 50.0 us)
Async XLA Ops:
  0.6 19.4 %copy-start.9 = (s32[256,8,4]{0,2,1:T(4,128)S(1)}, s32[256,8,4]{0,2,1:T(4,128)}, u32[]{:S(2)}) copy-start(s32[256,8,4]{0,2,1:T(4,128)} %param.15) | copy-start | bytes 98308
  0.6 20.4 %copy-start.4 = (bf16[64,4096]{1,0:T(8,128)(2,1)S(1)}, bf16[64,4096]{1,0:T(8,128)(2,1)}, u32[]{:S(2)}) copy-start(bf16[64,4096]{1,0:T(8,128)(2,1)} %param.9) | copy-start | bytes 1572868
  0.7 31.1 %copy-start.11 = (bf16[64,1024]{1,0:T(8,128)(2,1)S(1)}, bf16[64,1024]{1,0:T(8,128)(2,1)}, u32[]{:S(2)}) copy-start(bf16[64,1024]{1,0:T(8,128)(2,1)} %param.10) | copy-start | bytes 393220
  2.6 29.8 %copy-start.12 = (bf16[64,1024]{1,0:T(8,128)(2,1)S(1)}, bf16[64,1024]{1,0:T(8,128)(2,1)}, u32[]{:S(2)}) copy-start(bf16[64,1024]{1,0:T(8,128)(2,1)} %param.11) | copy-start | bytes 393220
  2.6 13.9 %all-to-all-start.2 = ((bf16[64,4,1024]{2,0,1:T(8,128)(2,1)}), bf16[64,4,1024]{2,0,1:T(8,128)(2,1)S(1)}, u32[]{:S(2)}, u32[]{:S(2)}) async-start(bf16[64,4,1024]{2,0,1:T(8,128)(2,1)} %bitcast.207), calls=%async_computation.2 | async-start | bytes 1048576 | tf_op jit(solution)/shard_map/all_to_all | solution.py:84
  16.5 11.7 %all-to-all-start.4 = ((bf16[64,4,1024]{2,0,1:T(8,128)(2,1)}), bf16[64,4,1024]{2,0,1:T(8,128)(2,1)S(1)}, u32[]{:S(2)}, u32[]{:S(2)}) async-start(bf16[64,4,1024]{2,0,1:T(8,128)(2,1)} %bitcast.206), calls=%async_computation.4 | async-start | bytes 1048576 | tf_op jit(solution)/shard_map/all_to_all | solution.py:85
  22.6 24.4 %copy-start.7 = (s32[128,64]{0,1:T(8,128)}, s32[128,64]{0,1:T(8,128)S(1)}, u32[]{:S(2)}) copy-start(s32[128,64]{0,1:T(8,128)S(1)} %convert_reduce_fusion.1) | copy-start | bytes 98308
  28.2 4.9 copy-start.1
  28.2 11.5 %all-to-all-start = ((bf16[64,4,1024]{2,0,1:T(8,128)(2,1)}), bf16[64,4,1024]{2,0,1:T(8,128)(2,1)S(1)}, u32[]{:S(2)}, u32[]{:S(2)}) async-start(bf16[64,4,1024]{2,0,1:T(8,128)(2,1)} %bitcast.208), calls=%async_computation | async-start | bytes 1048576 | tf_op jit(solution)/shard_map/all_to_all | solution.py:83
  31.7 56.6 %copy-start.13 = (s32[64]{0:T(128)}, s32[64]{0:T(128)S(1)}, u32[]{:S(2)}) copy-start(s32[64]{0:T(128)S(1)} %get-tuple-element.93) | copy-start | bytes 772
  39.8 9.3 %all-to-all-start.1 = ((bf16[64,4,256]{2,0,1:T(8,128)(2,1)}), bf16[64,4,256]{2,0,1:T(8,128)(2,1)S(1)}, u32[]{:S(2)}, u32[]{:S(2)}) async-start(bf16[64,4,256]{2,0,1:T(8,128)(2,1)} %bitcast.210), calls=%async_computation.1 | async-start | bytes 262144 | tf_op jit(solution)/shard_map/all_to_all | solution.py:86
  49.0 13.3 %all-to-all-start.3 = ((bf16[64,4,256]{2,0,1:T(8,128)(2,1)}), bf16[64,4,256]{2,0,1:T(8,128)(2,1)S(1)}, u32[]{:S(2)}, u32[]{:S(2)}) async-start(bf16[64,4,256]{2,0,1:T(8,128)(2,1)} %bitcast.264), calls=%async_computation.3 | async-start | bytes 262144 | tf_op jit(solution)/shard_map/all_to_all | solution.py:87
  62.4 37.9 %all-to-all-start.6 = ((f32[128,2,128]{2,1,0:T(2,128)}), f32[128,2,128]{2,1,0:T(2,128)S(1)}, u32[]{:S(2)}, u32[]{:S(2)}) async-start(f32[128,2,128]{2,1,0:T(2,128)} %scatter_fusion.1), calls=%async_computation.6 | async-start | bytes 262144 | tf_op jit(solution)/shard_map/all_to_all | solution.py:146
  100.3 15.5 %copy-start.8 = (s32[128,64]{0,1:T(8,128)S(1)}, s32[128,64]{0,1:T(8,128)}, u32[]{:S(2)}) copy-start(s32[128,64]{0,1:T(8,128)} %copy-done.7) | copy-start | bytes 98308
  100.3 16.4 %copy-start.10 = (s32[256,8,4]{0,2,1:T(4,128)S(1)}, s32[256,8,4]{0,2,1:T(4,128)}, u32[]{:S(2)}) copy-start(s32[256,8,4]{0,2,1:T(4,128)} %param.15) | copy-start | bytes 98308
  100.3 0.7 copy-start.5
  100.9 251.1 %all-to-all-start.5 = ((bf16[128,128,256]{2,1,0:T(8,128)(2,1)}), bf16[128,128,256]{2,1,0:T(8,128)(2,1)}, u32[]{:S(2)}, u32[]{:S(2)}) async-start(bf16[128,128,256]{2,1,0:T(8,128)(2,1)} %scatter_fusion), calls=%async_computation.5 | async-start | bytes 16777216 | tf_op jit(solution)/shard_map/all_to_all | solution.py:145
  115.9 10.7 %copy-start.18 = (s32[128]{0:T(128)}, s32[128]{0:T(128)S(1)}, u32[]{:S(2)}) copy-start(s32[128]{0:T(128)S(1)} %get-tuple-element.82) | copy-start | bytes 1540
  126.6 0.6 copy-start.20
  424.6 11.2 %copy-start.14 = (s32[64]{0:T(128)S(1)}, s32[64]{0:T(128)}, u32[]{:S(2)}) copy-start(s32[64]{0:T(128)} %copy-done.13) | copy-start | bytes 772
  424.6 12.4 %copy-start.19 = (s32[128]{0:T(128)S(1)}, s32[128]{0:T(128)}, u32[]{:S(2)}) copy-start(s32[128]{0:T(128)} %copy-done.18) | copy-start | bytes 1540
  424.6 12.4 %copy-start.21 = (s32[128]{0:T(128)S(1)}, s32[128]{0:T(128)}, u32[]{:S(2)}) copy-start(s32[128]{0:T(128)} %copy-done.20) | copy-start | bytes 1540
  424.6 113.4 %all-to-all-start.7 = ((bf16[128,128,128]{2,1,0:T(8,128)(2,1)}), bf16[128,128,128]{2,1,0:T(8,128)(2,1)}, u32[]{:S(2)}, u32[]{:S(2)}) async-start(bf16[128,128,128]{2,1,0:T(8,128)(2,1)} %bitcast.247), calls=%async_computation.7 | async-start | bytes 8388608 | tf_op jit(solution)/shard_map/all_to_all | solution.py:161
  437.5 2.6 copy-start.6
  438.3 2.7 copy-start.3
  438.6 2.3 copy-start
  441.4 4.1 copy-start.2
  449.9 6.9 %copy-start.15 = (s32[4,2]{0,1:T(2,128)S(1)}, s32[4,2]{0,1:T(2,128)}, u32[]{:S(2)}) copy-start(s32[4,2]{0,1:T(2,128)} %multiply_add_fusion) | copy-start | bytes 100
  449.9 6.9 %copy-start.16 = (pred[128]{0:T(512)(128)(4,1)S(1)}, pred[128]{0:T(512)(128)(4,1)}, u32[]{:S(2)}) copy-start(pred[128]{0:T(512)(128)(4,1)} %broadcast_compare_fusion.2) | copy-start | bytes 388
  449.9 6.9 %copy-start.17 = (s32[128]{0:T(128)S(1)}, s32[128]{0:T(128)}, u32[]{:S(2)}) copy-start(s32[128]{0:T(128)} %multiply_add_fusion.1) | copy-start | bytes 1540
  538.0 10.9 %all-to-all-start.10 = ((bf16[4,64,256]{2,1,0:T(8,128)(2,1)}), bf16[4,64,256]{2,1,0:T(8,128)(2,1)S(1)}, u32[]{:S(2)}, u32[]{:S(2)}) async-start(bf16[4,64,256]{2,1,0:T(8,128)(2,1)} %add_convert_fusion), calls=%async_computation.10 | async-start | bytes 262144 | tf_op jit(solution)/shard_map/all_to_all | solution.py:186
  548.8 9.3 %all-to-all-start.9 = ((bf16[4,64,256]{2,1,0:T(8,128)(2,1)}), bf16[4,64,256]{2,1,0:T(8,128)(2,1)S(1)}, u32[]{:S(2)}, u32[]{:S(2)}) async-start(bf16[4,64,256]{2,1,0:T(8,128)(2,1)} %add_convert_fusion.1), calls=%async_computation.9 | async-start | bytes 262144 | tf_op jit(solution)/shard_map/all_to_all | solution.py:185
  558.1 11.5 %all-to-all-start.8 = ((bf16[4,64,1024]{2,1,0:T(8,128)(2,1)}), bf16[4,64,1024]{2,1,0:T(8,128)(2,1)S(1)}, u32[]{:S(2)}, u32[]{:S(2)}) async-start(bf16[4,64,1024]{2,1,0:T(8,128)(2,1)} %all_to_all.122), calls=%async_computation.8 | async-start | bytes 1048576 | tf_op jit(solution)/shard_map/all_to_all | solution.py:184
where the time goes:
time: 574 us; the launch traced here: 570 us
  waiting for transfers between devices  326 us (57%)
  matrix products  75.3 us (13%)
  local copies, waits for them, and re-layouts  72.1 us (13%)
  starting transfers between devices  71.8 us (13%)
  other arithmetic  23.9 us (4%)
    all_to_all x1, waiting for transfers between devices, body(): lax.all_to_all(row_buffer, 'seq', split_axis=0, concat_axis=0, tiled=True)  220 us
    all_to_all x1, waiting for transfers between devices, body(): lax.all_to_all(dq_slots, 'seq', split_axis=0, concat_axis=0, tiled=True)  75.4 us
    all_to_all x1, starting transfers between devices, body(): lax.all_to_all(stat_buffer, 'seq', split_axis=0, concat_axis=0, tiled=True)  16.4 us
    dot_general x8, matrix products, remote_terms(): jnp.einsum('nkq,nqd->nkd', score_low, q_rows, preferred_element_type=jnp....  16.2 us
    dot_general x8, matrix products, remote_terms(): jnp.einsum('nkq,nqd->nkd', prob_low, o_grad, preferred_element_type=jnp.f...  16.1 us
    all_to_all x1, starting transfers between devices, body(): lax.all_to_all(row_buffer, 'seq', split_axis=0, concat_axis=0, tiled=True)  14.2 us
    dot_general x8, matrix products, remote_terms(): jnp.einsum('nkd,nqd->nkq', v_rows, o_grad, preferred_element_type=jnp.flo...  12.7 us
    dot_general x8, matrix products, remote_terms(): jnp.einsum('nkd,nqd->nkq', k_rows, q_rows, preferred_element_type=jnp.flo...  12.1 us
  transfers between devices with their start and end apart: 11, of which 9 were waited for; matrix products, arithmetic and copies ran while one was open for 16% of the time, Pallas kernels for 0%

commit v1 on v0

v1 whole, which is shorter than its diff:
```python
import functools
import math

import jax
import jax.numpy as jnp
from jax import lax
from jax.experimental import pallas as pl
from jax.experimental.pallas import tpu as pltpu
from jax.sharding import PartitionSpec as P

HD = 128
QB = 128
KB = 64
NSEL = 4
GROUP = 4
MESH = pl.DeviceIdType.MESH
SCALE = HD ** (-0.5)
UNROLL = 4


class Place:
    def __init__(self, R, X):
        self.R, self.X = R, X
        self.x = lax.axis_index("head")
        s = lax.axis_index("seq")
        self.c = s % 2
        self.z = (s // 2) % R
        self.y = s // (2 * R)
        self.qpos = self.qpos_of(self.c)
        self.kpos = self.qpos_of(1 - self.c)
        self.me = self.c * X + self.x

    def qpos_of(self, c):
        return c * self.y + (1 - c) * self.z

    def dev(self, y, z, c, x):
        return ((y * self.R + z) * 2 + c, x)

    def peer(self, j):
        c = (self.c + j % 2) % 2
        x = (self.x + j // 2) % self.X
        return c, x

    def peer_dev(self, j):
        c, x = self.peer(j)
        return self.dev(self.y, self.z, c, x)

    def src(self, j):
        c, x = self.peer(j)
        return c * self.X + x

    def q_next(self, d):
        d = d % self.R
        y = (self.y + self.c * d) % self.R
        z = (self.z + (1 - self.c) * d) % self.R
        return self.dev(y, z, self.c, self.x)

    def k_next(self, d):
        d = d % self.R
        y = (self.y + (1 - self.c) * d) % self.R
        z = (self.z + self.c * d) % self.R
        return self.dev(y, z, self.c, self.x)

    def barrier(self):
        sem = pltpu.get_barrier_semaphore()
        others = [self.peer_dev(j) for j in range(1, 2 * self.X)]
        others += [self.q_next(1), self.q_next(-1), self.k_next(1), self.k_next(-1)]
        for other in others:
            pl.semaphore_signal(sem, inc=1, device_id=other, device_id_type=MESH)
        pl.semaphore_wait(sem, len(others))


def gather_kernel(
    R, X, q, do, k, v, dl, ls, QD, KV, ST, xs, xr, ls_s, ls_r, loc, qs, qr, ks, kr, ss, sr
):
    p = Place(R, X)
    N = 2 * X
    K = R // 2
    p.barrier()

    def remote(src, dst, s_sem, r_sem, to):
        return pltpu.make_async_remote_copy(
            src_ref=src, dst_ref=dst, send_sem=s_sem, recv_sem=r_sem, device_id=to, device_id_type=MESH
        )

    def pieces(j):
        cj, xj = p.peer(j)
        kvh = 2 * xj + cj
        qcol = pl.ds(pl.multiple_of(kvh * (GROUP * HD), GROUP * HD), GROUP * HD)
        kcol = pl.ds(pl.multiple_of(kvh * HD, HD), HD)
        qp, kp = p.qpos_of(cj), p.qpos_of(1 - cj)
        return (
            (q.at[:, qcol], QD.at[qp, p.me, 0]),
            (do.at[:, qcol], QD.at[qp, p.me, 1]),
            (k.at[:, kcol], KV.at[kp, p.me, 0]),
            (v.at[:, kcol], KV.at[kp, p.me, 1]),
            (dl.at[kvh], ST.at[qp, p.me]),
        )

    def x_send(j, i):
        src, dst = pieces(j)[i]
        return remote(src, dst, xs.at[i, j], xr.at[i, p.me], p.peer_dev(j))

    def x_wait(j, i):
        n = p.src(j)
        dst = (QD.at[p.qpos, n, 0], QD.at[p.qpos, n, 1], KV.at[p.kpos, n, 0], KV.at[p.kpos, n, 1], ST.at[p.qpos, n])[i]
        remote(dst, dst, xs.at[i, j], xr.at[i, n], p.peer_dev(j)).wait_recv()

    other = p.dev(p.y, p.z, 1 - p.c, p.x)
    own_copies = [
        pltpu.make_async_copy(src, dst, loc.at[i]) for i, (src, dst) in enumerate(pieces(0))
    ]
    own_copies.append(pltpu.make_async_copy(ls.at[p.c], ST.at[p.qpos, N + p.c], loc.at[5]))
    for copy in own_copies:
        copy.start()
    for j in range(1, N):
        for i in range(5):
            x_send(j, i).start()
    oc = 1 - p.c
    ls_copy = remote(ls.at[oc], ST.at[p.qpos_of(oc), N + p.c], ls_s, ls_r, other)
    ls_copy.start()
    ls_back = remote(
        ST.at[p.qpos, N + oc], ST.at[p.qpos, N + oc], ls_s, ls_r, other
    )

    def q_copy(d, step, j):
        shift = R - (step - 1) if d == 0 else step - 1
        b = (p.qpos + shift) % R
        n = p.src(j)
        return remote(QD.at[b, n], QD.at[b, n], qs.at[d, step - 1, j], qr.at[d, step - 1, j], p.q_next(1 - 2 * d))

    def q_wait(d, step, j):
        shift = R - step if d == 0 else step
        b = (p.qpos + shift) % R
        n = p.src(j)
        remote(QD.at[b, n], QD.at[b, n], qs.at[d, step - 1, j], qr.at[d, step - 1, j], p.q_next(1 - 2 * d)).wait_recv()

    def k_copy(d, step, h):
        shift = R - (step - 1) if d == 0 else step - 1
        b = (p.kpos + shift) % R
        part = KV.at[b, pl.ds(h * X, X)]
        return remote(part, part, ks.at[d, step - 1, h], kr.at[d, step - 1, h], p.k_next(1 - 2 * d))

    def k_wait(d, step, h):
        shift = R - step if d == 0 else step
        b = (p.kpos + shift) % R
        part = KV.at[b, pl.ds(h * X, X)]
        remote(part, part, ks.at[d, step - 1, h], kr.at[d, step - 1, h], p.k_next(1 - 2 * d)).wait_recv()

    def s_copy(d, step):
        shift = R - (step - 1) if d == 0 else step - 1
        b = (p.qpos + shift) % R
        return remote(ST.at[b], ST.at[b], ss.at[d, step - 1], sr.at[d, step - 1], p.q_next(1 - 2 * d))

    def s_wait(d, step):
        shift = R - step if d == 0 else step
        b = (p.qpos + shift) % R
        remote(ST.at[b], ST.at[b], ss.at[d, step - 1], sr.at[d, step - 1], p.q_next(1 - 2 * d)).wait_recv()

    own_copies[0].wait()
    own_copies[1].wait()
    q_copy(0, 1, 0).start()
    q_copy(1, 1, 0).start()

    @pl.loop(1, N)
    def _(j):
        x_wait(j, 0)
        x_wait(j, 1)
        q_copy(0, 1, j).start()
        q_copy(1, 1, j).start()

    for copy in own_copies[2:]:
        copy.wait()

    @pl.loop(1, N)
    def _(j):
        for i in (2, 3, 4):
            x_wait(j, i)

    ls_back.wait_recv()
    for h in range(2):
        k_copy(0, 1, h).start()
        k_copy(1, 1, h).start()
    s_copy(0, 1).start()
    s_copy(1, 1).start()

    for step in range(2, K + 1):
        last = step == K

        def both(j, right=True, left=True, step=step):
            q_wait(0, step - 1, j)
            if right:
                q_copy(0, step, j).start()
            q_wait(1, step - 1, j)
            if left:
                q_copy(1, step, j).start()

        if not last:
            pl.loop(0, N)(both)
        else:
            pl.loop(0, X)(functools.partial(both, left=False))
            pl.loop(X, N)(functools.partial(both, right=False))
        for h in range(2):
            k_wait(0, step - 1, h)
            if not last or h == 0:
                k_copy(0, step, h).start()
            k_wait(1, step - 1, h)
            if not last or h == 1:
                k_copy(1, step, h).start()
        s_wait(0, step - 1)
        s_copy(0, step).start()
        s_wait(1, step - 1)
        if not last:
            s_copy(1, step).start()

    @pl.loop(0, X)
    def _(j):
        q_wait(0, K, j)
        q_wait(1, K, j + X)

    k_wait(0, K, 0)
    k_wait(1, K, 1)
    s_wait(0, K)

    @pl.loop(1, N)
    def _(j):
        for i in range(5):
            x_send(j, i).wait_send()

    ls_copy.wait_send()
    for step in range(1, K + 1):
        if step < K:

            @pl.loop(0, N)
            def _(j, step=step):
                q_copy(0, step, j).wait_send()
                q_copy(1, step, j).wait_send()

        else:

            @pl.loop(0, X)
            def _(j):
                q_copy(0, K, j).wait_send()
                q_copy(1, K, j + X).wait_send()

        for h in range(2):
            if step < K or h == 0:
                k_copy(0, step, h).wait_send()
            if step < K or h == 1:
                k_copy(1, step, h).wait_send()
        s_copy(0, step).wait_send()
        if step < K:
            s_copy(1, step).wait_send()


def gather(R, X, q, do, k, v, dl, ls):
    N, K = 2 * X, R // 2
    rows = q.shape[0]
    anyspace = pl.BlockSpec(memory_space=pl.ANY)
    dma = pltpu.SemaphoreType.DMA
    return pl.pallas_call(
        functools.partial(gather_kernel, R, X),
        out_shape=(
            jax.ShapeDtypeStruct((R, N, 2, rows, GROUP * HD), jnp.bfloat16),
            jax.ShapeDtypeStruct((R, N, 2, rows, HD), jnp.bfloat16),
            jax.ShapeDtypeStruct((R, N + 2, 8, 128), jnp.float32),
        ),
        in_specs=[anyspace] * 6,
        out_specs=(anyspace,) * 3,
        scratch_shapes=[
            dma((5, N)),
            dma((5, N)),
            dma,
            dma,
            dma((6,)),
            dma((2, K, N)),
            dma((2, K, N)),
            dma((2, K, 2)),
            dma((2, K, 2)),
            dma((2, K)),
            dma((2, K)),
        ],
        compiler_params=pltpu.CompilerParams(collective_id=1, has_side_effects=True),
        name="gather_rings",
    )(q, do, k, v, dl, ls)


def dot(a, b, ca, cb):
    return lax.dot_general(a, b, (((ca,), (cb,)), ((), ())), preferred_element_type=jnp.float32)


def pair_kernel(X, pairs, info, QD, KV, ST, dq_out, kv_out, oq, okv, dq, dkv):
    R, N = QD.shape[0], QD.shape[1]
    c, qpos, kpos, count = info[0], info[1], info[2], info[3]
    half = QB // 2

    @pl.loop(0, R * N)
    def _(i):
        dq[i // N, i % N] = jnp.zeros(dq.shape[2:], jnp.float32)
        dkv[i // N, i % N] = jnp.zeros(dkv.shape[2:], jnp.float32)

    def heads(p, s0, g):
        return pl.ds(s0, 2), pl.ds(pl.multiple_of(g * HD, HD), HD)

    def load_query(p, s0, g):
        rows, cols = heads(p, s0, g)
        qv = QD[p, rows, 0, :, cols].reshape(QB, HD)
        dov = QD[p, rows, 1, :, cols].reshape(QB, HD)
        b = (s0 // 2) % 2
        shard = s0 // X
        lse = ST[p, N + shard, pl.ds(b * GROUP + g, 1), :]
        delta = ST[p, s0, pl.ds(g, 1), :] + ST[p, s0 + 1, pl.ds(g, 1), :]
        return qv, dov, lse, delta

    def grads(qv, dov, lse, delta, kv, vv, mask=None):
        prob = jnp.exp(dot(kv, qv, 1, 1) * SCALE - lse)
        if mask is not None:
            prob = jnp.where(mask, prob, 0.0)
        ds = (prob * (dot(vv, dov, 1, 1) - delta)).astype(jnp.bfloat16)
        pb = prob.astype(jnp.bfloat16)
        return dot(ds, kv, 0, 0), dot(ds, qv, 1, 0), dot(pb, dov, 1, 0)

    causal = lax.broadcasted_iota(jnp.int32, (QB, QB), 0) <= lax.broadcasted_iota(jnp.int32, (QB, QB), 1)

    @pl.loop(0, N // 2)
    def _(blk):
        s0 = blk * 2
        kv = KV[kpos, pl.ds(s0, 2), 0].reshape(QB, HD)
        vv = KV[kpos, pl.ds(s0, 2), 1].reshape(QB, HD)
        results = []
        for g in range(GROUP):
            results.append(grads(*load_query(qpos, s0, g), kv, vv, causal))
        for g in range(GROUP):
            dq[qpos, pl.ds(s0, 2), :, g * HD : (g + 1) * HD] = results[g][0].reshape(2, half, HD)
        dkv[kpos, pl.ds(s0, 2), 0] = sum(r[1] for r in results).reshape(2, half, HD)
        dkv[kpos, pl.ds(s0, 2), 1] = sum(r[2] for r in results).reshape(2, half, HD)

    @pl.loop(0, (count + UNROLL - 1) // UNROLL)
    def _(t):
        results = []
        for u in range(UNROLL):
            i = t * UNROLL + u
            code = pairs[i]
            unit, key = code // (R * N), code % (R * N)
            g = unit % GROUP
            blk = unit // GROUP
            p, s0 = blk // (N // 2), (blk % (N // 2)) * 2
            kp, kn = key // N, key % N
            qv, dov, lse, delta = load_query(p, s0, g)
            lse = lse + jnp.where(i < count, 0.0, 1e30)
            out = grads(qv, dov, lse, delta, KV[kp, kn, 0], KV[kp, kn, 1])
            results.append((p, s0, g, kp, kn, out))
        for p, s0, g, kp, kn, out in results:
            rows, cols = heads(p, s0, g)
            dq[p, rows, :, cols] += out[0].reshape(2, half, HD)
            dkv[kp, kn, 0] += out[1]
            dkv[kp, kn, 1] += out[2]

    @pl.loop(0, R * N)
    def _(i):
        dq_out[i // N, i % N] = (dq[i // N, i % N] * SCALE).astype(jnp.bfloat16)
        kv_out[i // N, i % N, 0] = (dkv[i // N, i % N, 0] * SCALE).astype(jnp.bfloat16)
        kv_out[i // N, i % N, 1] = dkv[i // N, i % N, 1].astype(jnp.bfloat16)

    @pl.loop(0, N)
    def _(n):
        oq[n] = dq[qpos, n] * SCALE
        okv[n, 0] = dkv[kpos, n, 0] * SCALE
        okv[n, 1] = dkv[kpos, n, 1]


def pair_grads(X, pairs, info, QD, KV, ST):
    vmem = pl.BlockSpec(memory_space=pltpu.VMEM)
    smem = pl.BlockSpec(memory_space=pltpu.SMEM)
    q_shape = QD.shape[:2] + QD.shape[3:]
    return pl.pallas_call(
        functools.partial(pair_kernel, X),
        out_shape=(
            jax.ShapeDtypeStruct(q_shape, jnp.bfloat16),
            jax.ShapeDtypeStruct(KV.shape, jnp.bfloat16),
            jax.ShapeDtypeStruct(q_shape[1:], jnp.float32),
            jax.ShapeDtypeStruct(KV.shape[1:], jnp.float32),
        ),
        in_specs=[smem, smem, vmem, vmem, vmem],
        out_specs=(vmem,) * 4,
        scratch_shapes=[pltpu.VMEM(q_shape, jnp.float32), pltpu.VMEM(KV.shape, jnp.float32)],
        compiler_params=pltpu.CompilerParams(vmem_limit_bytes=50 << 20),
        name="pair_grads",
    )(pairs, info, QD, KV, ST)


def reduce_kernel(
    R, X, dq, dkv, oq, okv, gq, gk, gv, rq, rk, bq, bk, xs, xr, loc, qs, qr, ks, kr
):
    p = Place(R, X)
    N = 2 * X
    K = R // 2
    p.barrier()

    def remote(src, dst, s_sem, r_sem, to):
        return pltpu.make_async_remote_copy(
            src_ref=src, dst_ref=dst, send_sem=s_sem, recv_sem=r_sem, device_id=to, device_id_type=MESH
        )

    def owner(pos, d, step):
        far = K + 1 - step
        return (pos + (far if d == 0 else R - far)) % R

    def q_send(src, d, step, j):
        return remote(src, rq.at[d, step - 1, j], qs.at[d, step - 1, j], qr.at[d, step - 1, j], p.q_next(1 - 2 * d))

    def q_wait(d, step, j):
        buf = rq.at[d, step - 1, j]
        q_send(buf, d, step, j).wait_recv()

    def k_send(src, d, step, h):
        return remote(src, rk.at[d, step - 1, h], ks.at[d, step - 1, h], kr.at[d, step - 1, h], p.k_next(1 - 2 * d))

    def k_wait(d, step, h):
        buf = rk.at[d, step - 1, h]
        k_send(buf, d, step, h).wait_recv()

    def q_add(d, step, j):
        q_wait(d, step - 1, j)
        buf = rq.at[d, step - 2, j]
        mine = dq[owner(p.qpos, d, step), p.src(j)]
        buf[...] = (buf[...].astype(jnp.float32) + mine.astype(jnp.float32)).astype(jnp.bfloat16)
        q_send(buf, d, step, j).start()

    def q_plain(d, step, j):
        q_send(dq.at[owner(p.qpos, d, step), p.src(j)], d, step, j).start()

    def k_add(d, step, h):
        k_wait(d, step - 1, h)
        buf = rk.at[d, step - 2, h]
        mine = dkv[owner(p.kpos, d, step), pl.ds(h * X, X)]
        buf[...] = (buf[...].astype(jnp.float32) + mine.astype(jnp.float32)).astype(jnp.bfloat16)
        k_send(buf, d, step, h).start()

    def k_plain(d, step, h):
        k_send(dkv.at[owner(p.kpos, d, step), pl.ds(h * X, X)], d, step, h).start()

    @pl.loop(0, X)
    def _(j):
        q_plain(0, 1, j)
        q_plain(1, 1, j + X)

    k_plain(0, 1, 0)
    k_plain(1, 1, 1)

    @pl.loop(0, X)
    def _(j):
        q_plain(0, 2, j + X)
        q_plain(1, 2, j)

    k_plain(0, 2, 1)
    k_plain(1, 2, 0)

    @pl.loop(0, X)
    def _(j):
        q_add(0, 2, j)
        q_add(1, 2, j + X)

    k_add(0, 2, 0)
    k_add(1, 2, 1)

    for step in range(3, K + 1):

        @pl.loop(0, N)
        def _(j, step=step):
            q_add(0, step, (j + X) % N)
            q_add(1, step, j)

        for h in range(2):
            k_add(0, step, 1 - h)
            k_add(1, step, h)

    qcol = pl.ds(pl.multiple_of((2 * p.x + p.c) * (GROUP * HD), GROUP * HD), GROUP * HD)
    kcol = pl.ds(pl.multiple_of((2 * p.x + p.c) * HD, HD), HD)

    def x_copies(j):
        n = p.src(j)
        return (
            (bq.at[n], gq.at[:, qcol]),
            (bk.at[n, 0], gk.at[:, kcol]),
            (bk.at[n, 1], gv.at[:, kcol]),
        )

    def x_send(j, i):
        src, dst = x_copies(j)[i]
        return remote(src, dst, xs.at[i, j], xr.at[i, p.me], p.peer_dev(j))

    def q_total(j):
        q_wait(0, K, j)
        q_wait(1, K, j)
        n = p.src(j)
        bq[n] = (oq[n] + rq[0, K - 1, j].astype(jnp.float32) + rq[1, K - 1, j].astype(jnp.float32)).astype(jnp.bfloat16)

    @pl.loop(1, N)
    def _(j):
        q_total(j)
        x_send(j, 0).start()

    q_total(0)
    own = [pltpu.make_async_copy(src, dst, loc.at[i]) for i, (src, dst) in enumerate(x_copies(0))]
    own[0].start()
    for h in range(2):
        k_wait(0, K, h)
        k_wait(1, K, h)
        part = pl.ds(h * X, X)
        bk[part] = (
            okv[part] + rk[0, K - 1, h].astype(jnp.float32) + rk[1, K - 1, h].astype(jnp.float32)
        ).astype(jnp.bfloat16)

    @pl.loop(1, N)
    def _(j):
        x_send(j, 1).start()
        x_send(j, 2).start()

    own[1].start()
    own[2].start()

    def x_wait(j, i):
        cj, xj = p.peer(j)
        n = p.src(j)
        qc = pl.ds(pl.multiple_of((2 * xj + cj) * (GROUP * HD), GROUP * HD), GROUP * HD)
        kc = pl.ds(pl.multiple_of((2 * xj + cj) * HD, HD), HD)
        dst = (gq.at[:, qc], gk.at[:, kc], gv.at[:, kc])[i]
        src = (bq.at[n], bk.at[n, 0], bk.at[n, 1])[i]
        remote(src, dst, xs.at[i, j], xr.at[i, n], p.peer_dev(j)).wait_recv()

    @pl.loop(1, N)
    def _(j):
        for i in range(3):
            x_wait(j, i)
            x_send(j, i).wait_send()

    for copy in own:
        copy.wait()

    @pl.loop(0, X)
    def _(j):
        q_plain_wait(q_send, rq, 1, j, X)

    for step in range(2, K + 1):

        @pl.loop(0, N)
        def _(j, step=step):
            for d in range(2):
                q_send(rq.at[d, step - 1, j], d, step, j).wait_send()

    k_send(rk.at[0, 0, 0], 0, 1, 0).wait_send()
    k_send(rk.at[1, 0, 1], 1, 1, 1).wait_send()
    for step in range(2, K + 1):
        for h in range(2):
            for d in range(2):
                k_send(rk.at[d, step - 1, h], d, step, h).wait_send()


def q_plain_wait(q_send, rq, step, j, X):
    q_send(rq.at[0, step - 1, j], 0, step, j).wait_send()
    q_send(rq.at[1, step - 1, j + X], 1, step, j + X).wait_send()


def reduce(R, X, dq, dkv, oq, okv):
    N, K = 2 * X, R // 2
    rows = dq.shape[2]
    anyspace = pl.BlockSpec(memory_space=pl.ANY)
    vmem = pl.BlockSpec(memory_space=pltpu.VMEM)
    dma = pltpu.SemaphoreType.DMA
    return pl.pallas_call(
        functools.partial(reduce_kernel, R, X),
        out_shape=(
            jax.ShapeDtypeStruct((rows, N * GROUP * HD), jnp.bfloat16),
            jax.ShapeDtypeStruct((rows, N * HD), jnp.bfloat16),
            jax.ShapeDtypeStruct((rows, N * HD), jnp.bfloat16),
        ),
        in_specs=[vmem] * 4,
        out_specs=(anyspace,) * 3,
        scratch_shapes=[
            pltpu.VMEM((2, K, N) + dq.shape[2:], jnp.bfloat16),
            pltpu.VMEM((2, K, 2, X) + dkv.shape[2:], jnp.bfloat16),
            pltpu.VMEM(oq.shape, jnp.bfloat16),
            pltpu.VMEM(okv.shape, jnp.bfloat16),
            dma((3, N)),
            dma((3, N)),
            dma((3,)),
            dma((2, K, N)),
            dma((2, K, N)),
            dma((2, K, 2)),
            dma((2, K, 2)),
        ],
        compiler_params=pltpu.CompilerParams(
            collective_id=2, has_side_effects=True, vmem_limit_bytes=40 << 20
        ),
        name="reduce_rings",
    )(dq, dkv, oq, okv)


def list_pairs(R, X, block_lists):
    s = lax.axis_index("seq")
    c, z, y = s % 2, (s // 2) % R, s // (2 * R)
    lists = block_lists.reshape(R, R, 2, 2, 2, GROUP * NSEL)
    lists = lax.dynamic_index_in_dim(lists, c, 4, keepdims=False)
    along_z = lax.dynamic_index_in_dim(lists, y, 0, keepdims=False)
    along_y = lax.dynamic_index_in_dim(lists, z, 1, keepdims=False)
    mine = jnp.where(c == 0, along_z, along_y).reshape(-1)
    per_shard = X
    shard, local = mine // per_shard, mine % per_shard
    ky, kz, kc = shard // (2 * R), (shard // 2) % R, shard % 2
    here = jnp.where(c == 0, kz == z, ky == y)
    kp = jnp.where(c == 0, ky, kz)
    n = mine.shape[0]
    unit = jnp.arange(n, dtype=jnp.int32) // NSEL
    code = unit * (R * 2 * X) + kp * (2 * X) + kc * X + local
    ids = jnp.arange(n, dtype=jnp.int32)
    rank = jnp.sum((here[None, :] & (ids[None, :] < ids[:, None])).astype(jnp.int32), axis=1)
    hit = (rank[None, :] == ids[:, None]) & here[None, :]
    packed = jnp.sum(jnp.where(hit, code[None, :], 0), axis=1)
    count = jnp.sum(here.astype(jnp.int32))
    qpos, kpos = c * y + (1 - c) * z, c * z + (1 - c) * y
    return packed, jnp.stack([c, qpos, kpos, count]).astype(jnp.int32)


def body(R, X, queries, keys, values, outputs_saved, grad_out, lse, block_lists):
    rows = queries.shape[0]
    x = lax.axis_index("head")
    products = grad_out.astype(jnp.float32) * outputs_saved.astype(jnp.float32)
    delta = jnp.sum(products.reshape(rows, -1, HD), axis=-1).T
    delta = delta.reshape(2 * X, GROUP, rows)
    none = jnp.zeros_like(delta)
    odd = x % 2 == 1
    delta = jnp.concatenate([jnp.where(odd, none, delta), jnp.where(odd, delta, none)], axis=-1)
    delta = jnp.pad(delta, ((0, 0), (0, 8 - GROUP), (0, 0)))
    stats = lse.reshape(2, QB, 2, GROUP).transpose(2, 0, 3, 1).reshape(2, 2 * GROUP, QB)
    QD, KV, ST = gather(R, X, queries, grad_out, keys, values, delta, stats)
    pairs, info = list_pairs(R, X, block_lists)
    dq, dkv, oq, okv = pair_grads(X, pairs, info, QD, KV, ST)
    return reduce(R, X, dq, dkv, oq, okv)


def solution(mesh):
    R = math.isqrt(mesh.shape["seq"] // 2)
    X = mesh.shape["head"]
    in_specs = (
        P(("seq", "head"), None),
        P(("seq", "head"), None),
        P(("seq", "head"), None),
        P(("seq", "head"), None),
        P(("seq", "head"), None),
        P("seq", "head"),
        P(None, "head", None),
    )
    out_specs = (P(("seq", "head"), None), P(("seq", "head"), None), P(("seq", "head"), None))
    return jax.shard_map(
        functools.partial(body, R, X), mesh=mesh, in_specs=in_specs, out_specs=out_specs, check_vma=False
    )
```

time: 574 us -> 178 us (0.31)
  the two profiles are of different devices: /device:TPU:96 before, /device:TPU:1 now
where the time goes in v1:
time: 178 us
  Pallas kernels  164 us (92%)
  local copies, waits for them, and re-layouts  7.92 us (4%)
  other arithmetic  4.71 us (3%)
    pallas_call x1, Pallas kernels, gather(): pl.pallas_call(functools.partial(gather_kernel, R, X), out_shape=(jax.Sha...  81.1 us
    pallas_call x1, Pallas kernels, reduce(): pl.pallas_call(functools.partial(reduce_kernel, R, X), out_shape=(jax.Sha...  47.5 us
    pallas_call x1, Pallas kernels, pair_grads(): pl.pallas_call(functools.partial(pair_kernel, X), out_shape=(jax.ShapeDty...  35.5 us
    unnamed x11, local copies, waits for them, and re-layouts  5.89 us

profile of v1, /device:TPU:1, one launch (start us, length us, event | category | flops | bytes accessed | tf_op | source)
XLA Modules:
  0.0 177.5 jit_solution(9347486315110788560)
XLA Ops:
  0.6 0.0 copy-start.2
  0.7 0.7 reshape.147
  1.4 0.6 copy.20
  2.0 1.3 multiply_bitcast_fusion
  3.4 0.2 copy.21
  3.5 0.3 reduce_sum.39
  3.9 0.1 copy.18
  4.0 0.1 copy.19
  4.0 0.7 select_maximum_fusion.dl
  4.8 0.0 copy-done.2
  4.8 0.4 copy.17
  5.2 0.3 reshape.145
  5.6 0.1 dynamic-slice_reduce_fusion
  5.6 1.1 fusion.3
  6.7 0.1 squeeze.13
  6.8 0.8 pad_add_fusion.info
  7.5 0.1 squeeze.12
  7.7 0.1 convert_reduce_fusion
  7.9 0.3 select_reduce_fusion.pairs
  8.2 81.1 %gather_rings.1 = (bf16[8,8,2,64,512]{4,3,2,1,0:T(8,128)(2,1)}, bf16[8,8,2,64,128]{4,3,2,1,0:T(8,128)(2,1)}, f32[8,10,8,128]{3,2,1,0:T(8,128)}) custom-call(bf16[64,4096]{1,0:T(8,128)(2,1)} %q.1, bf16[64,4096]{1,0:T(8,128)(2,1)} %do.1, bf16[64,1024]{1,0:T(8,128)(2,1)} %k.1, bf16[64,1024]{1,0:T(8,128)(2,1)} %v.1, f32[8,8,128]{2,1,0:T(8,128)} %select_maximum_fusion.dl, ...), custom_call_target="tpu_custom_call" | custom-call | tf_op jit(solution)/shard_map/gather_rings/pallas_call | solution.py:261
  89.2 0.0 copy-start.1
  89.2 1.0 copy-done.1
  90.2 35.5 %pair_grads.1 = (bf16[8,8,64,512]{3,2,1,0:T(8,128)(2,1)}, bf16[8,8,2,64,128]{4,3,2,1,0:T(8,128)(2,1)S(1)}, f32[8,64,512]{2,1,0:T(8,128)S(1)}, f32[8,2,64,128]{3,2,1,0:T(8,128)S(1)}) custom-call(s32[512]{0:T(512)S(1)} %select_reduce_fusion.pairs, s32[4]{0:T(128)S(1)} %pad_add_fusion.info, bf16[8,8,2,64,512]{4,3,2,1,0:T(8,128)(2,1)} %get-tuple-element.10.QD, ...), custom_call_target="tpu_custom_call" | custom-call | tf_op jit(solution)/shard_map/pair_grads/pallas_call | solution.py:376
  125.7 0.0 copy-start
  125.7 2.2 %copy-done = bf16[8,8,64,512]{3,2,1,0:T(8,128)(2,1)S(1)} copy-done((bf16[8,8,64,512]{3,2,1,0:T(8,128)(2,1)S(1)}, bf16[8,8,64,512]{3,2,1,0:T(8,128)(2,1)}, u32[]{:S(2)}) %copy-start) | copy-done | bytes 4194328
  127.9 47.5 %reduce_rings.1 = (bf16[64,4096]{1,0:T(8,128)(2,1)S(1)}, bf16[64,1024]{1,0:T(8,128)(2,1)S(1)}, bf16[64,1024]{1,0:T(8,128)(2,1)S(1)}) custom-call(bf16[8,8,64,512]{3,2,1,0:T(8,128)(2,1)S(1)} %copy-done, bf16[8,8,2,64,128]{4,3,2,1,0:T(8,128)(2,1)S(1)} %get-tuple-element.14.dkv, f32[8,64,512]{2,1,0:T(8,128)S(1)} %get-tuple-element.15.oq, ...), custom_call_target="tpu_custom_call" | custom-call | tf_op jit(solution)/shard_map/reduce_rings/pallas_call | solution.py:571
  175.4 0.8 copy.25
  176.2 0.7 copy.26
  176.9 0.7 copy.27
  (3 shorter events, 0.1 us)
Async XLA Ops:
  0.6 4.1 %copy-start.2 = (s32[256,8,4]{0,2,1:T(4,128)S(1)}, s32[256,8,4]{0,2,1:T(4,128)}, u32[]{:S(2)}) copy-start(s32[256,8,4]{0,2,1:T(4,128)} %param.13) | copy-start | bytes 98308
  89.2 1.0 copy-start.1
  125.7 2.2 %copy-start = (bf16[8,8,64,512]{3,2,1,0:T(8,128)(2,1)S(1)}, bf16[8,8,64,512]{3,2,1,0:T(8,128)(2,1)}, u32[]{:S(2)}) copy-start(bf16[8,8,64,512]{3,2,1,0:T(8,128)(2,1)} %get-tuple-element.13.dq) | copy-start | bytes 12582916

commit v2 on v0

v2 whole, which is shorter than its diff:
```python
import functools
import math

import jax
import jax.numpy as jnp
from jax import lax
from jax.experimental import pallas as pl
from jax.experimental.pallas import tpu as pltpu
from jax.sharding import PartitionSpec as P

HD = 128
QB = 128
KB = 64
NSEL = 4
GROUP = 4
WIDE = GROUP * HD
MESH = pl.DeviceIdType.MESH
SCALE = HD ** (-0.5)
UNROLL = 4


class Place:
    def __init__(self, R, X):
        self.R, self.X = R, X
        self.x = lax.axis_index("head")
        s = lax.axis_index("seq")
        self.c = s % 2
        self.z = (s // 2) % R
        self.y = s // (2 * R)

    def dev(self, dx=0, dy=0, dz=0):
        return self.at((self.x + dx) % self.X, (self.y + dy) % self.R, (self.z + dz) % self.R)

    def at(self, x, y, z):
        return ((y * self.R + z) * 2 + self.c, x)

    def sibling(self):
        return ((self.y * self.R + self.z) * 2 + 1 - self.c, self.x)

    def far(self, t):
        return ((t % 2) * ((t + 1) // 2) + (1 - t % 2) * (self.R - t // 2)) % self.R

    def barrier(self):
        sem = pltpu.get_barrier_semaphore()
        others = [self.dev(dx=dx, dy=dy) for dx in range(self.X) for dy in range(self.R) if dx or dy]
        others += [self.dev(dz=1), self.dev(dz=self.R - 1), self.sibling()]
        for other in others:
            pl.semaphore_signal(sem, inc=1, device_id=other, device_id_type=MESH)
        pl.semaphore_wait(sem, len(others))


def remote(src, dst, s_sem, r_sem, to):
    return pltpu.make_async_remote_copy(
        src_ref=src, dst_ref=dst, send_sem=s_sem, recv_sem=r_sem, device_id=to, device_id_type=MESH
    )


def dot(a, b, ca, cb):
    return lax.dot_general(a, b, (((ca,), (cb,)), ((), ())), preferred_element_type=jnp.float32)


def columns(g):
    return pl.ds(pl.multiple_of(g * HD, HD), HD)


def load_query(QD, DL, LS, n, b, g):
    rows, cols = pl.ds(2 * b, 2), columns(g)
    qv = QD[rows, n, 0, :, cols].reshape(QB, HD)
    dov = QD[rows, n, 1, :, cols].reshape(QB, HD)
    lse = LS[n, pl.ds(b * GROUP + g, 1), :]
    delta = DL[2 * b, n, pl.ds(g, 1), :] + DL[2 * b + 1, n, pl.ds(g, 1), :]
    return qv, dov, lse, delta


def grads(qv, dov, lse, delta, kv, vv, mask=None):
    prob = jnp.exp(dot(kv, qv, 1, 1) * SCALE - lse)
    if mask is not None:
        prob = jnp.where(mask, prob, 0.0)
    ds = (prob * (dot(vv, dov, 1, 1) - delta)).astype(jnp.bfloat16)
    pb = prob.astype(jnp.bfloat16)
    return dot(ds, kv, 0, 0), dot(ds, qv, 1, 0), dot(pb, dov, 1, 0)


def gather_kernel(
    R, X, q, do, o, k, v, ls, QD, KV, DL, LS, LI, dq0, dkv0, dl, do_v, o_v,
    ys, yr, ls_s, ls_r, loc, qs, qr, fs, fr, ds, dr, ks, kr, ms, mr,
):
    p = Place(R, X)
    K = R // 2
    H = R // 2
    x, y, z, c = p.x, p.y, p.z, p.c
    loads = [
        pltpu.make_async_copy(src, dst, loc.at[6 + i])
        for i, (src, dst) in enumerate(((do, do_v), (o, o_v)))
    ]
    for copy in loads:
        copy.start()
    p.barrier()

    def pieces(t):
        head = (y + p.far(t)) % R
        qcol = pl.ds(pl.multiple_of(head * WIDE, WIDE), WIDE)
        kcol = pl.ds(pl.multiple_of(head * HD, HD), HD)
        return (
            (k.at[:, kcol], KV.at[c, z, y, 0]),
            (v.at[:, kcol], KV.at[c, z, y, 1]),
            (q.at[:, qcol], QD.at[x, y, 0]),
            (do.at[:, qcol], QD.at[x, y, 1]),
            (dl.at[head], DL.at[x, y]),
        )

    def y_send(t, i):
        src, dst = pieces(t)[i]
        return remote(src, dst, ys.at[i, t], yr.at[i, y], p.dev(dy=p.far(t)))

    def y_wait(t, i):
        n = (y + p.far(t)) % R
        dst = (KV.at[c, z, n, 0], KV.at[c, z, n, 1], QD.at[x, n, 0], QD.at[x, n, 1], DL.at[x, n])[i]
        remote(dst, dst, ys.at[i, t], yr.at[i, n], p.dev(dy=p.far(t))).wait_recv()

    own = [pltpu.make_async_copy(src, dst, loc.at[i]) for i, (src, dst) in enumerate(pieces(0))]
    for copy in own[:4]:
        copy.start()

    def y_start(t, kinds):
        for i in kinds:
            y_send(t, i).start()

    y_start(1, (2, 3))
    y_start(2, (2, 3))

    @pl.loop(1, R)
    def _(t):
        y_start(t, (0, 1))

    def ls_send(i, dx):
        return remote(
            ls.at[i], LS.at[y], ls_s.at[i, dx], ls_r.at[y], p.at((x + dx) % X, 2 * x + i, z)
        )

    ls_home = y // 2 == x
    ls_own = pltpu.make_async_copy(ls.at[y % 2], LS.at[y], loc.at[5])

    def ls_each(act):
        for i in range(2):
            for dx in range(X):
                if dx:
                    act(ls_send(i, dx))
                else:
                    pl.when(y != 2 * x + i)(functools.partial(act, ls_send(i, dx)))

    ls_each(lambda copy: copy.start())
    pl.when(ls_home)(ls_own.start)

    at_head = lax.broadcasted_iota(jnp.int32, (8, HD), 0)
    picks = [(at_head == g).astype(jnp.bfloat16) for g in range(GROUP)]
    lane = lax.broadcasted_iota(jnp.int32, (8, QB), 1)
    here = (lane // KB) == x % 2

    for copy in loads:
        copy.wait()

    @pl.loop(0, R)
    def _(n):
        cols = pl.ds(pl.multiple_of(n * WIDE, WIDE), WIDE)
        prod = do_v[:, cols].astype(jnp.float32) * o_v[:, cols].astype(jnp.float32)
        high = prod.astype(jnp.bfloat16)
        low = (prod - high.astype(jnp.float32)).astype(jnp.bfloat16)
        tile = jnp.zeros((8, KB), jnp.float32)
        for g in range(GROUP):
            at = slice(g * HD, (g + 1) * HD)
            tile += dot(picks[g], high[:, at], 1, 1) + dot(picks[g], low[:, at], 1, 1)
        dl[n] = jnp.where(here, jnp.concatenate([tile, tile], axis=1), 0.0)

    own[4].start()

    @pl.loop(1, R)
    def _(t):
        y_start(t, (4,))

    @pl.loop(3, R)
    def _(t):
        y_start(t, (2, 3))

    def q_send(d, t):
        n = (y + p.far(t)) % R
        part = QD.at[x, n]
        return remote(part, part, qs.at[d, t], qr.at[d, t], p.dev(dx=1 if d == 0 else X - 1))

    def q_arrived(d, t):
        n = (y + p.far(t)) % R
        part = QD.at[(x + (X - 1 if d == 0 else 1)) % X, n]
        remote(part, part, qs.at[d, t], qr.at[d, t], p.dev(dx=1 if d == 0 else X - 1)).wait_recv()

    def f_send(d, t):
        n = (y + p.far(t)) % R
        part = QD.at[(x + (X - 1 if d == 0 else 1)) % X, n, d]
        return remote(part, part, fs.at[d, t], fr.at[d, t], p.dev(dx=1 if d == 0 else X - 1))

    def f_arrived(d, t):
        n = (y + p.far(t)) % R
        part = QD.at[(x + 2) % X, n, d]
        remote(part, part, fs.at[d, t], fr.at[d, t], p.dev(dx=1 if d == 0 else X - 1)).wait_recv()

    def d_send(d, hop):
        part = DL.at[(x + (0, X - 1 if d == 0 else 1)[hop]) % X]
        return remote(part, part, ds.at[d, hop], dr.at[d, hop], p.dev(dx=1 if d == 0 else X - 1))

    def d_arrived(d, hop):
        part = DL.at[(x + (X - 1 if d == 0 else 1, 2)[hop]) % X]
        remote(part, part, ds.at[d, hop], dr.at[d, hop], p.dev(dx=1 if d == 0 else X - 1)).wait_recv()

    def k_block(d, hops):
        return (z + (R - hops if d == 0 else hops)) % R

    def k_send(d, step, h):
        part = KV.at[c, k_block(d, step - 1), pl.ds(h * H, H)]
        return remote(part, part, ks.at[d, step - 1, h], kr.at[d, step - 1, h], p.dev(dz=1 if d == 0 else R - 1))

    def k_arrived(d, step, h):
        part = KV.at[c, k_block(d, step), pl.ds(h * H, H)]
        remote(
            part, part, ks.at[d, step - 1, h], kr.at[d, step - 1, h], p.dev(dz=1 if d == 0 else R - 1)
        ).wait_recv()

    def mirror(b):
        return remote(KV.at[c, b], KV.at[c, b], ms.at[b], mr.at[b], p.sibling())

    def mirrored(b):
        part = KV.at[1 - c, b]
        remote(part, part, ms.at[b], mr.at[b], p.sibling()).wait_recv()

    def k_first():
        own[0].wait()
        own[1].wait()

        @pl.loop(1, R)
        def _(t):
            y_wait(t, 0)
            y_wait(t, 1)

        for h in range(2):
            k_send(0, 1, h).start()
            k_send(1, 1, h).start()
        mirror(z).start()

    def k_step(step):
        for h in range(2):
            k_arrived(0, step - 1, h)
            if step < K or h == 0:
                k_send(0, step, h).start()
            k_arrived(1, step - 1, h)
            if step < K or h == 1:
                k_send(1, step, h).start()
        mirror(k_block(0, step - 1)).start()
        mirror(k_block(1, step - 1)).start()

    def spread(t):
        for d in range(2):
            q_send(d, t).start()

    def forward(t):
        for d in range(2):
            q_arrived(d, t)
            f_send(d, t).start()

    def d_first():
        own[4].wait()

        @pl.loop(1, R)
        def _(t):
            y_wait(t, 4)

        d_send(0, 0).start()
        d_send(1, 0).start()

    def d_second():
        d_arrived(0, 0)
        d_send(0, 1).start()
        d_arrived(1, 0)

    def stats_arrived():
        @pl.loop(1, R)
        def _(t):
            n = (y + t) % R
            remote(LS.at[n], LS.at[n], ls_s.at[0, 0], ls_r.at[n], p.dev(dy=1)).wait_recv()

        pl.when(ls_home)(ls_own.wait)

        @pl.when(jnp.logical_not(ls_home))
        def _():
            remote(LS.at[y], LS.at[y], ls_s.at[0, 0], ls_r.at[y], p.dev(dy=1)).wait_recv()

        LI[...] = LS[:, 2 * GROUP, :]

    key_at = lax.broadcasted_iota(jnp.int32, (KB, QB), 0) + (x % 2) * KB
    causal = key_at <= lax.broadcasted_iota(jnp.int32, (KB, QB), 1)

    def own_terms(t):
        n = (y + p.far(t)) % R
        kv, vv = KV[c, z, n, 0], KV[c, z, n, 1]
        results = [grads(*load_query(QD, DL, LS, n, x // 2, g), kv, vv, causal) for g in range(GROUP)]
        for g in range(GROUP):
            dq0[:, n, :, g * HD : (g + 1) * HD] = results[g][0].reshape(2, KB, HD)
        dkv0[n, 0] = sum(r[1] for r in results)
        dkv0[n, 1] = sum(r[2] for r in results)

    own[2].wait()
    own[3].wait()
    spread(0)
    for t in range(1, R):
        y_wait(t, 2)
        y_wait(t, 3)
        spread(t)
        if t > 1:
            forward(t - 2)
        if t == 1:
            k_first()
        if t == 2:
            d_first()
            stats_arrived()
        if t == 3:
            d_second()
        if t in (3, 5, 7):
            k_step((t + 1) // 2)
        if t >= 4:
            for e in ((0, 1), (2, 3), (4,), (5,))[t - 4]:
                own_terms(e)

    forward(R - 2)
    forward(R - 1)
    own_terms(R - 2)
    own_terms(R - 1)
    k_arrived(0, K, 0)
    k_arrived(1, K, 1)
    mirror(k_block(0, K)).start()

    @pl.loop(0, R)
    def _(t):
        f_arrived(0, t)
        f_arrived(1, t)

    d_arrived(0, 1)

    @pl.loop(0, R)
    def _(b):
        mirrored(b)

    ls_each(lambda copy: copy.wait_send())

    @pl.loop(1, R)
    def _(t):
        for i in range(5):
            y_send(t, i).wait_send()

    @pl.loop(0, R)
    def _(t):
        for d in range(2):
            q_send(d, t).wait_send()
            f_send(d, t).wait_send()
        mirror(t).wait_send()

    d_send(0, 0).wait_send()
    d_send(1, 0).wait_send()
    d_send(0, 1).wait_send()
    for step in range(1, K + 1):
        for h in range(2):
            if step < K or h == 0:
                k_send(0, step, h).wait_send()
            if step < K or h == 1:
                k_send(1, step, h).wait_send()


def gather(R, X, q, do, o, k, v, ls):
    K = R // 2
    rows = q.shape[0]
    anyspace = pl.BlockSpec(memory_space=pl.ANY)
    vmem = pl.BlockSpec(memory_space=pltpu.VMEM)
    dma = pltpu.SemaphoreType.DMA
    f32 = jnp.float32
    return pl.pallas_call(
        functools.partial(gather_kernel, R, X),
        out_shape=(
            jax.ShapeDtypeStruct((X, R, 2, rows, WIDE), jnp.bfloat16),
            jax.ShapeDtypeStruct((2, R, R, 2, rows, HD), jnp.bfloat16),
            jax.ShapeDtypeStruct((X, R, 8, QB), f32),
            jax.ShapeDtypeStruct((R,) + ls.shape[1:], f32),
            jax.ShapeDtypeStruct((R, QB), f32),
            jax.ShapeDtypeStruct((2, R, rows, WIDE), f32),
            jax.ShapeDtypeStruct((R, 2, rows, HD), f32),
        ),
        in_specs=[pl.BlockSpec(memory_space=pltpu.HBM)] * 5 + [anyspace],
        out_specs=(vmem,) * 7,
        scratch_shapes=[
            pltpu.VMEM((R, 8, QB), f32),
            pltpu.VMEM(do.shape, do.dtype),
            pltpu.VMEM(o.shape, o.dtype),
            dma((5, R)),
            dma((5, R)),
            dma((2, X)),
            dma((R,)),
            dma((8,)),
            dma((2, R)),
            dma((2, R)),
            dma((2, R)),
            dma((2, R)),
            dma((2, 2)),
            dma((2, 2)),
            dma((2, K, 2)),
            dma((2, K, 2)),
            dma((R,)),
            dma((R,)),
        ],
        compiler_params=pltpu.CompilerParams(
            collective_id=1, has_side_effects=True, vmem_limit_bytes=20 << 20
        ),
        name="gather_rings",
    )(q, do, o, k, v, ls)


def pair_kernel(LI, QD, KV, DL, LS, dq0, dkv0, dq, dkv, pairs):
    X, R = QD.shape[:2]
    x = lax.axis_index("head")
    s = lax.axis_index("seq")
    c, z = s % 2, (s // 2) % R
    own_b = x // 2
    blocks = 2 * R * R
    listed = GROUP * NSEL

    def scan(i, count):
        dq[i // R, i % R] = jnp.zeros(dq.shape[2:], jnp.float32)
        for e in range(blocks // (X * R)):
            dkv[i * (blocks // (X * R)) + e] = jnp.zeros(dkv.shape[1:], jnp.float32)
        for e in range(2 * R * listed // (X * R)):
            k = i * (2 * R * listed // (X * R)) + e
            block = LI[k // (2 * listed), k % (2 * listed)].astype(jnp.int32)
            shard = block // X
            key = ((shard % 2) * R + shard // 2 % R) * R + shard // (2 * R)
            pairs[count] = (k // NSEL) * blocks + key
            count += (block % X == x).astype(jnp.int32)
        return count

    count = lax.fori_loop(0, X * R, scan, jnp.int32(0))
    for e in range(UNROLL):
        pairs[count + e] = 0

    @pl.loop(0, R)
    def _(n):
        dq[pl.ds(2 * own_b, 2), n] = dq0[:, n]
        dkv[(c * R + z) * R + n] = dkv0[n]

    @pl.loop(0, (count + UNROLL - 1) // UNROLL)
    def _(t):
        results = []
        for u in range(UNROLL):
            i = t * UNROLL + u
            code = pairs[i]
            unit, key = code // blocks, code % blocks
            g, b, n = unit % GROUP, unit // GROUP % 2, unit // (2 * GROUP)
            qv, dov, lse, delta = load_query(QD, DL, LS, n, b, g)
            lse = lse + jnp.where(i < count, 0.0, 1e30)
            results.append((n, b, g, key, grads(qv, dov, lse, delta, KV[key, 0], KV[key, 1])))
        for n, b, g, key, out in results:
            dq[pl.ds(2 * b, 2), n, :, columns(g)] += out[0].reshape(2, KB, HD)
            dkv[key, 0] += out[1]
            dkv[key, 1] += out[2]


def pair_grads(LI, QD, KV, DL, LS, dq0, dkv0):
    vmem = pl.BlockSpec(memory_space=pltpu.VMEM)
    smem = pl.BlockSpec(memory_space=pltpu.SMEM)
    X, R = QD.shape[:2]
    flat = KV.reshape((2 * R * R,) + KV.shape[3:])
    dq, dkv = pl.pallas_call(
        pair_kernel,
        out_shape=(
            jax.ShapeDtypeStruct(QD.shape[:2] + QD.shape[3:], jnp.float32),
            jax.ShapeDtypeStruct(flat.shape, jnp.float32),
        ),
        in_specs=[smem] + [vmem] * 6,
        out_specs=(vmem,) * 2,
        scratch_shapes=[pltpu.SMEM((2 * R * GROUP * NSEL + UNROLL,), jnp.int32)],
        compiler_params=pltpu.CompilerParams(vmem_limit_bytes=28 << 20),
        name="pair_grads",
    )(LI, QD, flat, DL, LS, dq0, dkv0)
    return dq, dkv.reshape(KV.shape)


def reduce_kernel(
    R, X, dq, dkv, gq, gk, gv, sf, sp, fq, rq, sm, mk, rk, bq, bk,
    ys, yr, loc, fs, fr, qs, qr, ms, mr, ks, kr,
):
    p = Place(R, X)
    K = R // 2
    H = R // 2
    x, y, z, c = p.x, p.y, p.z, p.c
    rows = dq.shape[2]
    half = rows // 2
    p.barrier()
    f32 = jnp.float32

    def piece(t):
        return (y + p.far(R - 1 - t)) % R

    def x_to(d):
        return p.dev(dx=1 if d == 0 else X - 1)

    def z_to(d):
        return p.dev(dz=1 if d == 0 else R - 1)

    def part_q(dx, n, at=slice(None)):
        return dq[(x + dx) % X, n, at] * SCALE

    def part_kv(core, b, at=slice(None)):
        part = dkv[core, b, at]
        return jnp.concatenate([part[:, :1] * SCALE, part[:, 1:]], axis=1)

    def f_send(d, t):
        return remote(sf.at[d, t], fq.at[d, t], fs.at[d, t], fr.at[d, t], x_to(d))

    def f_start(t):
        for d in range(2):
            sf[d, t] = part_q(2, piece(t), pl.ds(d * half, half)).astype(jnp.bfloat16)
            f_send(d, t).start()

    def q_send(d, t, late):
        src = (fq if late else sp).at[d, t]
        dst = rq.at[d, t, pl.ds((d if late else 1 - d) * half, half)]
        return remote(src, dst, qs.at[late, d, t], qr.at[late, d, t], x_to(d))

    def q_plain(t):
        for d in range(2):
            at = pl.ds((1 - d) * half, half)
            sp[d, t] = part_q(1 if d == 0 else X - 1, piece(t), at).astype(jnp.bfloat16)
            q_send(d, t, 0).start()

    def q_add(t):
        q_plain(t)
        for d in range(2):
            f_send(d, t).wait_recv()
            mine = part_q(1 if d == 0 else X - 1, piece(t), pl.ds(d * half, half))
            fq[d, t] = (mine + fq[d, t].astype(f32)).astype(jnp.bfloat16)
            q_send(d, t, 1).start()

    def mirror(b):
        return remote(sm.at[b], mk.at[b], ms.at[b], mr.at[b], p.sibling())

    def m_start(b):
        sm[b] = part_kv(1 - c, b).astype(jnp.bfloat16)
        mirror(b).start()

    def owner(d, step):
        far = K + 1 - step
        return (z + (far if d == 0 else R - far)) % R

    def k_send(d, step, h):
        src = mk.at[owner(d, step), pl.ds(h * H, H)]
        return remote(src, rk.at[d, step - 1, h], ks.at[d, step - 1, h], kr.at[d, step - 1, h], z_to(d))

    def k_step(step):
        for d in range(2):
            b = owner(d, step)
            if step > 1 or d == 0:
                mirror(b).wait_recv()
            for h in range(2):
                if step == 1 and h != d:
                    continue
                at = pl.ds(h * H, H)
                total = mk[b, at].astype(f32) + part_kv(c, b, at)
                if step > 2 or (step == 2 and h == d):
                    k_send(d, step - 1, h).wait_recv()
                    total = total + rk[d, step - 2, h].astype(f32)
                mk[b, at] = total.astype(jnp.bfloat16)
                k_send(d, step, h).start()

    m_start((z + K) % R)
    pl.loop(0, R)(f_start)
    for far in range(K - 1, 0, -1):
        m_start((z + far) % R)
        m_start((z + R - far) % R)
    m_start(z)

    def out_refs(n, head):
        qcol = pl.ds(pl.multiple_of(head * WIDE, WIDE), WIDE)
        kcol = pl.ds(pl.multiple_of(head * HD, HD), HD)
        return (
            (bq.at[n], gq.at[:, qcol]),
            (bk.at[n, 0], gk.at[:, kcol]),
            (bk.at[n, 1], gv.at[:, kcol]),
        )

    def y_send(t, i):
        src, dst = out_refs(piece(t), y)[i]
        return remote(src, dst, ys.at[i, t], yr.at[i, y], p.dev(dy=p.far(R - 1 - t)))

    def y_wait(t, i):
        n = piece(t)
        src, dst = out_refs(n, n)[i]
        remote(src, dst, ys.at[i, t], yr.at[i, n], p.dev(dy=p.far(R - 1 - t))).wait_recv()

    own = [pltpu.make_async_copy(src, dst, loc.at[i]) for i, (src, dst) in enumerate(out_refs(y, y))]

    def q_total(t):
        for d in range(2):
            q_send(d, t, 0).wait_recv()
            q_send(d, t, 1).wait_recv()
        n = piece(t)
        bq[n] = (part_q(0, n) + rq[0, t].astype(f32) + rq[1, t].astype(f32)).astype(jnp.bfloat16)

    def q_home(t):
        q_total(t)
        y_send(t, 0).start()

    k_step(1)
    pl.loop(0, H)(q_add)
    k_step(2)
    pl.loop(H, R)(q_add)
    k_step(3)
    pl.loop(0, H)(q_home)
    for step in range(4, K + 1):
        k_step(step)
    pl.loop(H, R - 1)(q_home)
    q_total(R - 1)
    own[0].start()
    mirror(z).wait_recv()
    for h in range(2):
        at = pl.ds(h * H, H)
        total = part_kv(c, z, at) + mk[z, at].astype(f32)
        for d in range(2):
            k_send(d, K, h).wait_recv()
            total = total + rk[d, K - 1, h].astype(f32)
        bk[at] = total.astype(jnp.bfloat16)

    @pl.loop(0, R - 1)
    def _(t):
        y_send(t, 1).start()
        y_send(t, 2).start()

    own[1].start()
    own[2].start()

    @pl.loop(0, R - 1)
    def _(t):
        for i in range(3):
            y_wait(t, i)

    for copy in own:
        copy.wait()

    @pl.loop(0, R - 1)
    def _(t):
        for i in range(3):
            y_send(t, i).wait_send()

    @pl.loop(0, R)
    def _(t):
        for d in range(2):
            f_send(d, t).wait_send()
            q_send(d, t, 0).wait_send()
            q_send(d, t, 1).wait_send()
        mirror(t).wait_send()

    for step in range(1, K + 1):
        for h in range(2):
            for d in range(2):
                if step > 1 or h == d:
                    k_send(d, step, h).wait_send()


def reduce(R, X, dq, dkv):
    K = R // 2
    rows = dq.shape[2]
    anyspace = pl.BlockSpec(memory_space=pl.ANY)
    vmem = pl.BlockSpec(memory_space=pltpu.VMEM)
    dma = pltpu.SemaphoreType.DMA
    bf16 = jnp.bfloat16
    return pl.pallas_call(
        functools.partial(reduce_kernel, R, X),
        out_shape=(
            jax.ShapeDtypeStruct((rows, R * WIDE), bf16),
            jax.ShapeDtypeStruct((rows, R * HD), bf16),
            jax.ShapeDtypeStruct((rows, R * HD), bf16),
        ),
        in_specs=[vmem] * 2,
        out_specs=(anyspace,) * 3,
        scratch_shapes=[
            pltpu.VMEM((2, R, rows // 2, WIDE), bf16),
            pltpu.VMEM((2, R, rows // 2, WIDE), bf16),
            pltpu.VMEM((2, R, rows // 2, WIDE), bf16),
            pltpu.VMEM((2, R, rows, WIDE), bf16),
            pltpu.VMEM(dkv.shape[1:], bf16),
            pltpu.VMEM(dkv.shape[1:], bf16),
            pltpu.VMEM((2, K, 2, R // 2) + dkv.shape[3:], bf16),
            pltpu.VMEM(dq.shape[1:], bf16),
            pltpu.VMEM(dkv.shape[2:], bf16),
            dma((3, R)),
            dma((3, R)),
            dma((3,)),
            dma((2, R)),
            dma((2, R)),
            dma((2, 2, R)),
            dma((2, 2, R)),
            dma((R,)),
            dma((R,)),
            dma((2, K, 2)),
            dma((2, K, 2)),
        ],
        compiler_params=pltpu.CompilerParams(
            collective_id=2, has_side_effects=True, vmem_limit_bytes=26 << 20
        ),
        name="reduce_rings",
    )(dq, dkv)


def body(R, X, queries, keys, values, outputs_saved, grad_out, lse, block_lists):
    stats = lse.reshape(2, QB, 2, GROUP).transpose(2, 0, 3, 1).reshape(2, 2 * GROUP, QB)
    lists = lax.dynamic_slice_in_dim(block_lists, 2 * lax.axis_index("seq"), 2, 0)
    lists = lists.reshape(2, 2, GROUP, NSEL).transpose(1, 0, 2, 3).reshape(2, 1, 2 * GROUP * NSEL)
    lists = jnp.pad(lists.astype(jnp.float32), ((0, 0), (0, 7), (0, QB - 2 * GROUP * NSEL)))
    stats = jnp.concatenate([stats, lists], axis=1)
    QD, KV, DL, LS, LI, dq0, dkv0 = gather(
        R, X, queries, grad_out, outputs_saved, keys, values, stats
    )
    dq, dkv = pair_grads(LI, QD, KV, DL, LS, dq0, dkv0)
    return reduce(R, X, dq, dkv)


def solution(mesh):
    R = math.isqrt(mesh.shape["seq"] // 2)
    X = mesh.shape["head"]
    in_specs = (
        P(("seq", "head"), None),
        P(("seq", "head"), None),
        P(("seq", "head"), None),
        P(("seq", "head"), None),
        P(("seq", "head"), None),
        P("seq", "head"),
        P(None, "head", None),
    )
    out_specs = (P(("seq", "head"), None), P(("seq", "head"), None), P(("seq", "head"), None))
    return jax.shard_map(
        functools.partial(body, R, X), mesh=mesh, in_specs=in_specs, out_specs=out_specs, check_vma=False
    )
```

time: 574 us -> 154 us (0.27)
  the two profiles are of different devices: /device:TPU:96 before, /device:TPU:1 now
where the time goes in v2:
time: 154 us
  Pallas kernels  145 us (94%)
  local copies, waits for them, and re-layouts  8.25 us (5%)
    pallas_call x1, Pallas kernels, gather(): pl.pallas_call(functools.partial(gather_kernel, R, X), out_shape=(jax.Sha...  66.5 us
    pallas_call x1, Pallas kernels, reduce(): pl.pallas_call(functools.partial(reduce_kernel, R, X), out_shape=(jax.Sha...  52.4 us
    pallas_call x1, Pallas kernels, pair_grads(): pl.pallas_call(pair_kernel, out_shape=(jax.ShapeDtypeStruct(QD.shape[:2]...  26.2 us
    unnamed x16, local copies, waits for them, and re-layouts  7.18 us

profile of v2, /device:TPU:1, one launch (start us, length us, event | category | flops | bytes accessed | tf_op | source)
XLA Modules:
  0.0 154.1 jit_solution(15766315512090462622)
XLA Ops:
  0.6 0.0 copy-start
  0.7 0.7 reshape.34
  1.4 0.0 copy-done
  1.4 0.1 constant_dynamic-slice_fusion
  1.5 0.1 copy.18
  1.6 0.1 convert_element_type.23
  1.7 0.1 copy.16
  1.8 0.1 convert_element_type.25
  1.9 0.0 copy-start.1
  1.9 1.0 copy-done.1
  2.9 0.0 copy-start.2
  2.9 1.0 copy-done.2
  4.0 0.0 copy-start.3
  4.0 1.0 copy-done.3
  5.0 0.0 copy-start.4
  5.0 0.9 copy-done.4
  5.9 0.0 copy-start.5
  5.9 0.9 copy-done.5
  6.8 66.5 %gather_rings.1 = (bf16[4,8,2,64,512]{4,3,2,1,0:T(8,128)(2,1)S(1)}, bf16[2,8,8,2,64,128]{5,4,3,2,1,0:T(8,128)(2,1)S(1)}, f32[4,8,8,128]{3,2,1,0:T(8,128)S(1)}, f...) custom-call(bf16[64,4096]{1,0:T(8,128)(2,1)S(1)} %copy-done.1, ...), custom_call_target="tpu_custom_call" | custom-call | tf_op jit(solution)/shard_map/gather_rings/pallas_call | solution.py:381
  73.3 26.2 %pair_grads.1 = (f32[4,8,64,512]{3,2,1,0:T(8,128)S(1)}, f32[128,2,64,128]{3,2,1,0:T(8,128)S(1)}) custom-call(f32[8,128]{1,0:T(8,128)S(1)} %get-tuple-element.12.LI, bf16[4,8,2,64,512]{4,3,2,1,0:T(8,128)(2,1)S(1)} %get-tuple-element.13.QD, bf16[128,2,64,128]{3,2,1,0:T(8,128)(2,1)S(1)} %bitcast.12, f32[4,8,8,128]{3,2,1,0:T(8,128)S(1)} %get-tuple-element.15.DL, ...), custom_call_target="tpu_custom_call" | custom-call | tf_op jit(solution)/shard_map/pair_grads/pallas_call | solution.py:474
  99.6 52.4 %reduce_rings.1 = (bf16[64,4096]{1,0:T(8,128)(2,1)S(1)}, bf16[64,1024]{1,0:T(8,128)(2,1)S(1)}, bf16[64,1024]{1,0:T(8,128)(2,1)S(1)}) custom-call(f32[4,8,64,512]{3,2,1,0:T(8,128)S(1)} %get-tuple-element.19.dq, f32[2,8,8,2,64,128]{5,4,3,2,1,0:T(8,128)S(1)} %bitcast.11), custom_call_target="tpu_custom_call" | custom-call | tf_op jit(solution)/shard_map/reduce_rings/pallas_call | solution.py:677
  152.0 0.8 copy.22
  152.8 0.7 copy.23
  153.4 0.7 copy.24
  (3 shorter events, 0.0 us)
Async XLA Ops:
  0.6 0.8 copy-start
  1.9 1.0 copy-start.1
  2.9 1.0 copy-start.2
  4.0 1.0 copy-start.3
  5.0 0.9 copy-start.4
  5.9 0.9 copy-start.5

commit v3 on v2

--- a/solution.py
+++ b/solution.py
@@ -17,6 +17,7 @@
 MESH = pl.DeviceIdType.MESH
 SCALE = HD ** (-0.5)
 UNROLL = 4
+PARTS = 4
 
 
 class Place:
@@ -59,6 +60,14 @@
     return lax.dot_general(a, b, (((ca,), (cb,)), ((), ())), preferred_element_type=jnp.float32)
 
 
+def quot(a, n):
+    return lax.shift_right_logical(a, jnp.int32(n.bit_length() - 1))
+
+
+def rest(a, n):
+    return a & jnp.int32(n - 1)
+
+
 def columns(g):
     return pl.ds(pl.multiple_of(g * HD, HD), HD)
 
@@ -73,10 +82,11 @@
 
 
 def grads(qv, dov, lse, delta, kv, vv, mask=None):
-    prob = jnp.exp(dot(kv, qv, 1, 1) * SCALE - lse)
+    both = dot(jnp.concatenate([kv, vv], axis=0), jnp.concatenate([qv, dov], axis=0), 1, 1)
+    prob = jnp.exp(both[:KB, :QB] * SCALE - lse)
     if mask is not None:
         prob = jnp.where(mask, prob, 0.0)
-    ds = (prob * (dot(vv, dov, 1, 1) - delta)).astype(jnp.bfloat16)
+    ds = (prob * (both[KB:, QB:] - delta)).astype(jnp.bfloat16)
     pb = prob.astype(jnp.bfloat16)
     return dot(ds, kv, 0, 0), dot(ds, qv, 1, 0), dot(pb, dov, 1, 0)
 
@@ -389,7 +399,7 @@
             jax.ShapeDtypeStruct((2, R, rows, WIDE), f32),
             jax.ShapeDtypeStruct((R, 2, rows, HD), f32),
         ),
-        in_specs=[pl.BlockSpec(memory_space=pltpu.HBM)] * 5 + [anyspace],
+        in_specs=[anyspace] * 6,
         out_specs=(vmem,) * 7,
         scratch_shapes=[
             pltpu.VMEM((R, 8, QB), f32),
@@ -415,7 +425,7 @@
             collective_id=1, has_side_effects=True, vmem_limit_bytes=20 << 20
         ),
         name="gather_rings",
-    )(q, do, o, k, v, ls)
+    )(*(pltpu.with_memory_space_constraint(a, pltpu.HBM) for a in (q, do, o, k, v)), ls)
 
 
 def pair_kernel(LI, QD, KV, DL, LS, dq0, dkv0, dq, dkv, pairs):
@@ -433,11 +443,11 @@
             dkv[i * (blocks // (X * R)) + e] = jnp.zeros(dkv.shape[1:], jnp.float32)
         for e in range(2 * R * listed // (X * R)):
             k = i * (2 * R * listed // (X * R)) + e
-            block = LI[k // (2 * listed), k % (2 * listed)].astype(jnp.int32)
-            shard = block // X
-            key = ((shard % 2) * R + shard // 2 % R) * R + shard // (2 * R)
-            pairs[count] = (k // NSEL) * blocks + key
-            count += (block % X == x).astype(jnp.int32)
+            block = LI[quot(k, 2 * listed), rest(k, 2 * listed)].astype(jnp.int32)
+            shard = quot(block, X)
+            key = (rest(shard, 2) * R + rest(quot(shard, 2), R)) * R + quot(shard, 2 * R)
+            pairs[count] = quot(k, NSEL) * blocks + key
+            count += (rest(block, X) == x).astype(jnp.int32)
         return count
 
     count = lax.fori_loop(0, X * R, scan, jnp.int32(0))
@@ -455,8 +465,8 @@
         for u in range(UNROLL):
             i = t * UNROLL + u
             code = pairs[i]
-            unit, key = code // blocks, code % blocks
-            g, b, n = unit % GROUP, unit // GROUP % 2, unit // (2 * GROUP)
+            unit, key = quot(code, blocks), rest(code, blocks)
+            g, b, n = rest(unit, GROUP), rest(quot(unit, GROUP), 2), quot(unit, 2 * GROUP)
             qv, dov, lse, delta = load_query(QD, DL, LS, n, b, g)
             lse = lse + jnp.where(i < count, 0.0, 1e30)
             results.append((n, b, g, key, grads(qv, dov, lse, delta, KV[key, 0], KV[key, 1])))
@@ -492,7 +502,7 @@
 ):
     p = Place(R, X)
     K = R // 2
-    H = R // 2
+    H = R // PARTS
     x, y, z, c = p.x, p.y, p.z, p.c
     rows = dq.shape[2]
     half = rows // 2
@@ -557,21 +567,30 @@
         src = mk.at[owner(d, step), pl.ds(h * H, H)]
         return remote(src, rk.at[d, step - 1, h], ks.at[d, step - 1, h], kr.at[d, step - 1, h], z_to(d))
 
-    def k_step(step):
-        for d in range(2):
-            b = owner(d, step)
-            if step > 1 or d == 0:
-                mirror(b).wait_recv()
-            for h in range(2):
-                if step == 1 and h != d:
-                    continue
-                at = pl.ds(h * H, H)
-                total = mk[b, at].astype(f32) + part_kv(c, b, at)
-                if step > 2 or (step == 2 and h == d):
-                    k_send(d, step - 1, h).wait_recv()
-                    total = total + rk[d, step - 2, h].astype(f32)
-                mk[b, at] = total.astype(jnp.bfloat16)
-                k_send(d, step, h).start()
+    def k_one(d, step, h):
+        b = owner(d, step)
+        at = pl.ds(h * H, H)
+        total = mk[b, at].astype(f32) + part_kv(c, b, at)
+        if step > 2 or (step == 2 and h // (PARTS // 2) == d):
+            k_send(d, step - 1, h).wait_recv()
+            total = total + rk[d, step - 2, h].astype(f32)
+        mk[b, at] = total.astype(jnp.bfloat16)
+        k_send(d, step, h).start()
+
+    def k_mirrored(step):
+        mirror(owner(0, step)).wait_recv()
+        if step > 1:
+            mirror(owner(1, step)).wait_recv()
+
+    def k_early(step):
+        for i in range(PARTS // 2):
+            k_one(0, step, PARTS // 2 + i)
+            k_one(1, step, i)
+
+    def k_late(step):
+        for i in range(PARTS // 2):
+            k_one(0, step, i)
+            k_one(1, step, PARTS // 2 + i)
 
     m_start((z + K) % R)
     pl.loop(0, R)(f_start)
@@ -611,33 +630,51 @@
         q_total(t)
         y_send(t, 0).start()
 
-    k_step(1)
-    pl.loop(0, H)(q_add)
-    k_step(2)
-    pl.loop(H, R)(q_add)
-    k_step(3)
-    pl.loop(0, H)(q_home)
-    for step in range(4, K + 1):
-        k_step(step)
-    pl.loop(H, R - 1)(q_home)
+    def k_out(n, i):
+        return remote(out_refs(n, y)[i][0], out_refs(n, y)[i][1], ys.at[i, n], yr.at[i, y], p.at(x, n, z))
+
+    def k_home(h):
+        at = pl.ds(h * H, H)
+        total = part_kv(c, z, at) + mk[z, at].astype(f32)
+        for d in range(2):
+            k_send(d, K, h).wait_recv()
+            total = total + rk[d, K - 1, h].astype(f32)
+        bk[at] = total.astype(jnp.bfloat16)
+
+        @pl.loop(h * H, (h + 1) * H)
+        def _(n):
+            @pl.when(n != y)
+            def _():
+                k_out(n, 1).start()
+                k_out(n, 2).start()
+
+            @pl.when(n == y)
+            def _():
+                own[1].start()
+                own[2].start()
+
+    k_mirrored(1)
+    k_late(1)
+    k_mirrored(2)
+    k_early(2)
+    pl.loop(0, 4)(q_add)
+    k_late(2)
+    pl.loop(4, R)(q_add)
+    k_mirrored(3)
+    k_early(3)
+    pl.loop(0, 2)(q_home)
+    k_late(3)
+    pl.loop(2, 4)(q_home)
+    k_mirrored(4)
+    k_early(4)
+    pl.loop(4, 6)(q_home)
+    k_late(4)
+    pl.loop(6, R - 1)(q_home)
     q_total(R - 1)
     own[0].start()
     mirror(z).wait_recv()
-    for h in range(2):
-        at = pl.ds(h * H, H)
-        total = part_kv(c, z, at) + mk[z, at].astype(f32)
-        for d in range(2):
-            k_send(d, K, h).wait_recv()
-            total = total + rk[d, K - 1, h].astype(f32)
-        bk[at] = total.astype(jnp.bfloat16)
-
-    @pl.loop(0, R - 1)
-    def _(t):
-        y_send(t, 1).start()
-        y_send(t, 2).start()
-
-    own[1].start()
-    own[2].start()
+    for h in range(PARTS):
+        k_home(h)
 
     @pl.loop(0, R - 1)
     def _(t):
@@ -649,8 +686,14 @@
 
     @pl.loop(0, R - 1)
     def _(t):
-        for i in range(3):
-            y_send(t, i).wait_send()
+        y_send(t, 0).wait_send()
+
+    @pl.loop(0, R)
+    def _(n):
+        @pl.when(n != y)
+        def _():
+            k_out(n, 1).wait_send()
+            k_out(n, 2).wait_send()
 
     @pl.loop(0, R)
     def _(t):
@@ -661,9 +704,9 @@
         mirror(t).wait_send()
 
     for step in range(1, K + 1):
-        for h in range(2):
+        for h in range(PARTS):
             for d in range(2):
-                if step > 1 or h == d:
+                if step > 1 or h // (PARTS // 2) == d:
                     k_send(d, step, h).wait_send()
 
 
@@ -690,7 +733,7 @@
             pltpu.VMEM((2, R, rows, WIDE), bf16),
             pltpu.VMEM(dkv.shape[1:], bf16),
             pltpu.VMEM(dkv.shape[1:], bf16),
-            pltpu.VMEM((2, K, 2, R // 2) + dkv.shape[3:], bf16),
+            pltpu.VMEM((2, K, PARTS, R // PARTS) + dkv.shape[3:], bf16),
             pltpu.VMEM(dq.shape[1:], bf16),
             pltpu.VMEM(dkv.shape[2:], bf16),
             dma((3, R)),
@@ -702,8 +745,8 @@
             dma((2, 2, R)),
             dma((R,)),
             dma((R,)),
-            dma((2, K, 2)),
-            dma((2, K, 2)),
+            dma((2, K, PARTS)),
+            dma((2, K, PARTS)),
         ],
         compiler_params=pltpu.CompilerParams(
             collective_id=2, has_side_effects=True, vmem_limit_bytes=26 << 20

time: 154 us -> 127 us (0.82); the launches traced: 154 us -> 125 us
  Pallas kernels: 145 us -> 121 us
  local copies, waits for them, and re-layouts: 8.25 us -> 3.32 us
    pallas_call x1, Pallas kernels: 26.2 us -> 12.3 us  [pair_grads(): pl.pallas_call(pair_kernel, out_shape=(jax.ShapeDtypeStruct(QD.shape[:2]...]
    pallas_call x1, Pallas kernels: 52.4 us -> 42.5 us  [reduce(): pl.pallas_call(functools.partial(reduce_kernel, R, X), out_shape=(jax.Sha...]
    unnamed x16 -> x6, local copies, waits for them, and re-layouts: 7.18 us -> 2.25 us
where the time goes in v3:
time: 127 us; the launch traced here: 125 us
  Pallas kernels  121 us (95%)
  local copies, waits for them, and re-layouts  3.32 us (3%)
    pallas_call x1, Pallas kernels, gather(): pl.pallas_call(functools.partial(gather_kernel, R, X), out_shape=(jax.Sha...  66.6 us
    pallas_call x1, Pallas kernels, reduce(): pl.pallas_call(functools.partial(reduce_kernel, R, X), out_shape=(jax.Sha...  42.5 us
    pallas_call x1, Pallas kernels, pair_grads(): pl.pallas_call(pair_kernel, out_shape=(jax.ShapeDtypeStruct(QD.shape[:2]...  12.3 us

profile of v3, /device:TPU:1, one launch (start us, length us, event | category | flops | bytes accessed | tf_op | source)
XLA Modules:
  0.0 125.5 jit_solution(1174497197545921996)
XLA Ops:
  0.6 0.0 copy-start
  0.7 0.7 reshape.34
  1.4 0.0 copy-done
  1.4 0.1 constant_dynamic-slice_fusion
  1.5 0.1 copy.18
  1.6 0.1 convert_element_type.23
  1.7 0.1 copy.16
  1.8 0.1 convert_element_type.25
  1.9 66.6 %gather_rings.1 = (bf16[4,8,2,64,512]{4,3,2,1,0:T(8,128)(2,1)S(1)}, bf16[2,8,8,2,64,128]{5,4,3,2,1,0:T(8,128)(2,1)S(1)}, f32[4,8,8,128]{3,2,1,0:T(8,128)S(1)}, f...) custom-call(bf16[64,4096]{1,0:T(8,128)(2,1)} %q.1, ...), custom_call_target="tpu_custom_call" | custom-call | tf_op jit(solution)/shard_map/gather_rings/pallas_call | solution.py:391
  68.5 12.3 %pair_grads.1 = (f32[4,8,64,512]{3,2,1,0:T(8,128)S(1)}, f32[128,2,64,128]{3,2,1,0:T(8,128)S(1)}) custom-call(f32[8,128]{1,0:T(8,128)S(1)} %get-tuple-element.12.LI, bf16[4,8,2,64,512]{4,3,2,1,0:T(8,128)(2,1)S(1)} %get-tuple-element.13.QD, bf16[128,2,64,128]{3,2,1,0:T(8,128)(2,1)S(1)} %bitcast.12, f32[4,8,8,128]{3,2,1,0:T(8,128)S(1)} %get-tuple-element.15.DL, ...), custom_call_target="tpu_custom_call" | custom-call | tf_op jit(solution)/shard_map/pair_grads/pallas_call | solution.py:484
  80.8 42.5 %reduce_rings.1 = (bf16[64,4096]{1,0:T(8,128)(2,1)S(1)}, bf16[64,1024]{1,0:T(8,128)(2,1)S(1)}, bf16[64,1024]{1,0:T(8,128)(2,1)S(1)}) custom-call(f32[4,8,64,512]{3,2,1,0:T(8,128)S(1)} %get-tuple-element.19.dq, f32[2,8,8,2,64,128]{5,4,3,2,1,0:T(8,128)S(1)} %bitcast.11), custom_call_target="tpu_custom_call" | custom-call | tf_op jit(solution)/shard_map/reduce_rings/pallas_call | solution.py:720
  123.3 0.8 copy.22
  124.1 0.7 copy.23
  124.8 0.7 copy.24
  (3 shorter events, 0.0 us)
Async XLA Ops:
  0.6 0.8 copy-start

commit v4 on v3

--- a/solution.py
+++ b/solution.py
@@ -41,9 +41,11 @@
     def far(self, t):
         return ((t % 2) * ((t + 1) // 2) + (1 - t % 2) * (self.R - t // 2)) % self.R
 
-    def barrier(self):
+    def barrier(self, plane):
         sem = pltpu.get_barrier_semaphore()
-        others = [self.dev(dx=dx, dy=dy) for dx in range(self.X) for dy in range(self.R) if dx or dy]
+        offsets = [(dx, dy) for dx in range(self.X) for dy in range(self.R) if dx or dy]
+        near = [(dx, dy) for dx, dy in offsets if not dx or (not dy and dx in (1, self.X - 1))]
+        others = [self.dev(dx=dx, dy=dy) for dx, dy in (offsets if plane else near)]
         others += [self.dev(dz=1), self.dev(dz=self.R - 1), self.sibling()]
         for other in others:
             pl.semaphore_signal(sem, inc=1, device_id=other, device_id_type=MESH)
@@ -105,7 +107,7 @@
     ]
     for copy in loads:
         copy.start()
-    p.barrier()
+    p.barrier(True)
 
     def pieces(t):
         head = (y + p.far(t)) % R
@@ -301,7 +303,12 @@
         def _():
             remote(LS.at[y], LS.at[y], ls_s.at[0, 0], ls_r.at[y], p.dev(dy=1)).wait_recv()
 
-        LI[...] = LS[:, 2 * GROUP, :]
+        lists = LS[:, 2 * GROUP, :]
+        shard = jnp.floor(lists / X)
+        chip = jnp.floor(shard / 2)
+        ky = jnp.floor(chip / R)
+        key = ((shard - 2 * chip) * R + chip - R * ky) * R + ky
+        LI[...] = jnp.where(lists - X * shard == x.astype(jnp.float32), key, -1.0).astype(jnp.int32)
 
     key_at = lax.broadcasted_iota(jnp.int32, (KB, QB), 0) + (x % 2) * KB
     causal = key_at <= lax.broadcasted_iota(jnp.int32, (KB, QB), 1)
@@ -395,7 +402,7 @@
             jax.ShapeDtypeStruct((2, R, R, 2, rows, HD), jnp.bfloat16),
             jax.ShapeDtypeStruct((X, R, 8, QB), f32),
             jax.ShapeDtypeStruct((R,) + ls.shape[1:], f32),
-            jax.ShapeDtypeStruct((R, QB), f32),
+            jax.ShapeDtypeStruct((R, QB), jnp.int32),
             jax.ShapeDtypeStruct((2, R, rows, WIDE), f32),
             jax.ShapeDtypeStruct((R, 2, rows, HD), f32),
         ),
@@ -443,11 +450,9 @@
             dkv[i * (blocks // (X * R)) + e] = jnp.zeros(dkv.shape[1:], jnp.float32)
         for e in range(2 * R * listed // (X * R)):
             k = i * (2 * R * listed // (X * R)) + e
-            block = LI[quot(k, 2 * listed), rest(k, 2 * listed)].astype(jnp.int32)
-            shard = quot(block, X)
-            key = (rest(shard, 2) * R + rest(quot(shard, 2), R)) * R + quot(shard, 2 * R)
+            key = LI[quot(k, 2 * listed), rest(k, 2 * listed)]
             pairs[count] = quot(k, NSEL) * blocks + key
-            count += (rest(block, X) == x).astype(jnp.int32)
+            count += (key >= 0).astype(jnp.int32)
         return count
 
     count = lax.fori_loop(0, X * R, scan, jnp.int32(0))
@@ -506,7 +511,7 @@
     x, y, z, c = p.x, p.y, p.z, p.c
     rows = dq.shape[2]
     half = rows // 2
-    p.barrier()
+    p.barrier(False)
     f32 = jnp.float32
 
     def piece(t):
@@ -673,8 +678,9 @@
     q_total(R - 1)
     own[0].start()
     mirror(z).wait_recv()
-    for h in range(PARTS):
-        k_home(h)
+    for i in range(PARTS // 2):
+        k_home(i)
+        k_home(PARTS // 2 + i)
 
     @pl.loop(0, R - 1)
     def _(t):
@@ -755,6 +761,28 @@
     )(dq, dkv)
 
 
+def finish_kernel(*refs):
+    n = len(refs) // 2
+    sems = refs[-1]
+    copies = [pltpu.make_async_copy(refs[i], refs[n + i], sems.at[i]) for i in range(n)]
+    for copy in copies:
+        copy.start()
+    for copy in copies:
+        copy.wait()
+
+
+def finish(*arrays):
+    anyspace = pl.BlockSpec(memory_space=pl.ANY)
+    return pl.pallas_call(
+        finish_kernel,
+        out_shape=tuple(jax.ShapeDtypeStruct(a.shape, a.dtype) for a in arrays),
+        in_specs=[anyspace] * len(arrays),
+        out_specs=(pl.BlockSpec(memory_space=pltpu.HBM),) * len(arrays),
+        scratch_shapes=[pltpu.SemaphoreType.DMA((len(arrays),))],
+        name="finish",
+    )(*arrays)
+
+
 def body(R, X, queries, keys, values, outputs_saved, grad_out, lse, block_lists):
     stats = lse.reshape(2, QB, 2, GROUP).transpose(2, 0, 3, 1).reshape(2, 2 * GROUP, QB)
     lists = lax.dynamic_slice_in_dim(block_lists, 2 * lax.axis_index("seq"), 2, 0)
@@ -765,7 +793,8 @@
         R, X, queries, grad_out, outputs_saved, keys, values, stats
     )
     dq, dkv = pair_grads(LI, QD, KV, DL, LS, dq0, dkv0)
-    return reduce(R, X, dq, dkv)
+    parts = reduce(R, X, dq, dkv)
+    return finish(*(pltpu.with_memory_space_constraint(a, pltpu.VMEM) for a in parts))
 
 
 def solution(mesh):

time: 127 us -> 123 us (0.969)
  local copies, waits for them, and re-layouts: 3.32 us -> 1.22 us
    pallas_call x1, Pallas kernels: 42.5 us -> 40.4 us  [reduce(): pl.pallas_call(functools.partial(reduce_kernel, R, X), out_shape=(jax.Sha...]
    unnamed x6 -> x3, local copies, waits for them, and re-layouts: 2.25 us -> 0.14 us
where the time goes in v4:
time: 123 us; the launch traced here: 121 us
  Pallas kernels  120 us (98%)
    pallas_call x1, Pallas kernels, gather(): pl.pallas_call(functools.partial(gather_kernel, R, X), out_shape=(jax.Sha...  66.6 us
    pallas_call x1, Pallas kernels, reduce(): pl.pallas_call(functools.partial(reduce_kernel, R, X), out_shape=(jax.Sha...  40.4 us
    pallas_call x1, Pallas kernels, pair_grads(): pl.pallas_call(pair_kernel, out_shape=(jax.ShapeDtypeStruct(QD.shape[:2]...  11.7 us

profile of v4, /device:TPU:1, one launch (start us, length us, event | category | flops | bytes accessed | tf_op | source)
XLA Modules:
  0.0 121.4 jit_solution(5728626025488549601)
XLA Ops:
  0.6 0.0 copy-start
  0.7 0.7 reshape.34
  1.4 0.0 copy-done
  1.4 0.1 constant_dynamic-slice_fusion
  1.5 0.1 copy.18
  1.6 0.1 convert_element_type.23
  1.7 0.1 copy.16
  1.8 0.1 convert_element_type.25
  1.9 66.6 %gather_rings.1 = (bf16[4,8,2,64,512]{4,3,2,1,0:T(8,128)(2,1)S(1)}, bf16[2,8,8,2,64,128]{5,4,3,2,1,0:T(8,128)(2,1)S(1)}, f32[4,8,8,128]{3,2,1,0:T(8,128)S(1)}, f...) custom-call(bf16[64,4096]{1,0:T(8,128)(2,1)} %q.1, ...), custom_call_target="tpu_custom_call" | custom-call | tf_op jit(solution)/shard_map/gather_rings/pallas_call | solution.py:398
  68.5 11.7 %pair_grads.1 = (f32[4,8,64,512]{3,2,1,0:T(8,128)S(1)}, f32[128,2,64,128]{3,2,1,0:T(8,128)S(1)}) custom-call(s32[8,128]{1,0:T(8,128)S(1)} %get-tuple-element.15.LI, bf16[4,8,2,64,512]{4,3,2,1,0:T(8,128)(2,1)S(1)} %get-tuple-element.16.QD, bf16[128,2,64,128]{3,2,1,0:T(8,128)(2,1)S(1)} %bitcast.12, f32[4,8,8,128]{3,2,1,0:T(8,128)S(1)} %get-tuple-element.18.DL, ...), custom_call_target="tpu_custom_call" | custom-call | tf_op jit(solution)/shard_map/pair_grads/pallas_call | solution.py:489
  80.1 40.4 %reduce_rings.1 = (bf16[64,4096]{1,0:T(8,128)(2,1)S(1)}, bf16[64,1024]{1,0:T(8,128)(2,1)S(1)}, bf16[64,1024]{1,0:T(8,128)(2,1)S(1)}) custom-call(f32[4,8,64,512]{3,2,1,0:T(8,128)S(1)} %get-tuple-element.22.dq, f32[2,8,8,2,64,128]{5,4,3,2,1,0:T(8,128)S(1)} %bitcast.11), custom_call_target="tpu_custom_call" | custom-call | tf_op jit(solution)/shard_map/reduce_rings/pallas_call | solution.py:726
  120.5 0.9 finish.1
  (3 shorter events, 0.0 us)
Async XLA Ops:
  0.6 0.8 copy-start

commit v5 on v4

--- a/solution.py
+++ b/solution.py
@@ -345,13 +345,12 @@
                 own_terms(e)
 
     forward(R - 2)
-    forward(R - 1)
-    own_terms(R - 2)
-    own_terms(R - 1)
     k_arrived(0, K, 0)
     k_arrived(1, K, 1)
     mirror(k_block(0, K)).start()
-
+    own_terms(R - 2)
+    forward(R - 1)
+    own_terms(R - 1)
     @pl.loop(0, R)
     def _(t):
         f_arrived(0, t)

time: 123 us -> 123 us (level)
  no operation moved by 1% of the time
where the time goes in v5:
time: 123 us; the launch traced here: 121 us
  Pallas kernels  119 us (97%)
    pallas_call x1, Pallas kernels, gather(): pl.pallas_call(functools.partial(gather_kernel, R, X), out_shape=(jax.Sha...  65.9 us
    pallas_call x1, Pallas kernels, reduce(): pl.pallas_call(functools.partial(reduce_kernel, R, X), out_shape=(jax.Sha...  40.3 us
    pallas_call x1, Pallas kernels, pair_grads(): pl.pallas_call(pair_kernel, out_shape=(jax.ShapeDtypeStruct(QD.shape[:2]...  12.2 us

profile of v5, /device:TPU:1, one launch (start us, length us, event | category | flops | bytes accessed | tf_op | source)
XLA Modules:
  0.0 121.1 jit_solution(2236378607786077114)
XLA Ops:
  0.6 0.0 copy-start
  0.7 0.7 reshape.34
  1.4 0.0 copy-done
  1.4 0.1 constant_dynamic-slice_fusion
  1.5 0.1 copy.18
  1.6 0.1 convert_element_type.23
  1.7 0.1 copy.16
  1.8 0.1 convert_element_type.25
  1.9 65.9 %gather_rings.1 = (bf16[4,8,2,64,512]{4,3,2,1,0:T(8,128)(2,1)S(1)}, bf16[2,8,8,2,64,128]{5,4,3,2,1,0:T(8,128)(2,1)S(1)}, f32[4,8,8,128]{3,2,1,0:T(8,128)S(1)}, f...) custom-call(bf16[64,4096]{1,0:T(8,128)(2,1)} %q.1, ...), custom_call_target="tpu_custom_call" | custom-call | tf_op jit(solution)/shard_map/gather_rings/pallas_call | solution.py:397
  67.8 12.2 %pair_grads.1 = (f32[4,8,64,512]{3,2,1,0:T(8,128)S(1)}, f32[128,2,64,128]{3,2,1,0:T(8,128)S(1)}) custom-call(s32[8,128]{1,0:T(8,128)S(1)} %get-tuple-element.15.LI, bf16[4,8,2,64,512]{4,3,2,1,0:T(8,128)(2,1)S(1)} %get-tuple-element.16.QD, bf16[128,2,64,128]{3,2,1,0:T(8,128)(2,1)S(1)} %bitcast.12, f32[4,8,8,128]{3,2,1,0:T(8,128)S(1)} %get-tuple-element.18.DL, ...), custom_call_target="tpu_custom_call" | custom-call | tf_op jit(solution)/shard_map/pair_grads/pallas_call | solution.py:488
  80.0 40.3 %reduce_rings.1 = (bf16[64,4096]{1,0:T(8,128)(2,1)S(1)}, bf16[64,1024]{1,0:T(8,128)(2,1)S(1)}, bf16[64,1024]{1,0:T(8,128)(2,1)S(1)}) custom-call(f32[4,8,64,512]{3,2,1,0:T(8,128)S(1)} %get-tuple-element.22.dq, f32[2,8,8,2,64,128]{5,4,3,2,1,0:T(8,128)S(1)} %bitcast.11), custom_call_target="tpu_custom_call" | custom-call | tf_op jit(solution)/shard_map/reduce_rings/pallas_call | solution.py:725
  120.2 0.9 finish.1
  (3 shorter events, 0.0 us)
Async XLA Ops:
  0.6 0.8 copy-start

commit v6 on v5

--- a/solution.py
+++ b/solution.py
@@ -783,7 +783,15 @@
 
 
 def body(R, X, queries, keys, values, outputs_saved, grad_out, lse, block_lists):
-    stats = lse.reshape(2, QB, 2, GROUP).transpose(2, 0, 3, 1).reshape(2, 2 * GROUP, QB)
+    heads = lse.T
+    stats = jnp.stack(
+        [
+            jnp.concatenate(
+                [heads[i * GROUP : (i + 1) * GROUP, b * QB : (b + 1) * QB] for b in range(2)], axis=0
+            )
+            for i in range(2)
+        ]
+    )
     lists = lax.dynamic_slice_in_dim(block_lists, 2 * lax.axis_index("seq"), 2, 0)
     lists = lists.reshape(2, 2, GROUP, NSEL).transpose(1, 0, 2, 3).reshape(2, 1, 2 * GROUP * NSEL)
     lists = jnp.pad(lists.astype(jnp.float32), ((0, 0), (0, 7), (0, QB - 2 * GROUP * NSEL)))

time: 123 us -> 123 us (level)
  no operation moved by 1% of the time
where the time goes in v6:
time: 123 us; the launch traced here: 121 us
  Pallas kernels  119 us (97%)
  local copies, waits for them, and re-layouts  1.25 us (1%)
    pallas_call x1, Pallas kernels, gather(): pl.pallas_call(functools.partial(gather_kernel, R, X), out_shape=(jax.Sha...  65.9 us
    pallas_call x1, Pallas kernels, reduce(): pl.pallas_call(functools.partial(reduce_kernel, R, X), out_shape=(jax.Sha...  40.8 us
    pallas_call x1, Pallas kernels, pair_grads(): pl.pallas_call(pair_kernel, out_shape=(jax.ShapeDtypeStruct(QD.shape[:2]...  11.7 us

profile of v6, /device:TPU:1, one launch (start us, length us, event | category | flops | bytes accessed | tf_op | source)
XLA Modules:
  0.0 121.2 jit_solution(17273831666547236070)
XLA Ops:
  0.6 0.0 copy-start
  0.7 0.8 fusion
  1.4 0.0 copy-done
  1.4 0.1 constant_dynamic-slice_fusion
  1.5 0.1 copy.16
  1.6 0.1 convert_element_type.23
  1.7 0.1 copy.14
  1.8 0.1 convert_element_type.25
  1.9 65.9 %gather_rings.1 = (bf16[4,8,2,64,512]{4,3,2,1,0:T(8,128)(2,1)S(1)}, bf16[2,8,8,2,64,128]{5,4,3,2,1,0:T(8,128)(2,1)S(1)}, f32[4,8,8,128]{3,2,1,0:T(8,128)S(1)}, f...) custom-call(bf16[64,4096]{1,0:T(8,128)(2,1)} %q.1, ...), custom_call_target="tpu_custom_call" | custom-call | tf_op jit(solution)/shard_map/gather_rings/pallas_call | solution.py:397
  67.9 11.7 %pair_grads.1 = (f32[4,8,64,512]{3,2,1,0:T(8,128)S(1)}, f32[128,2,64,128]{3,2,1,0:T(8,128)S(1)}) custom-call(s32[8,128]{1,0:T(8,128)S(1)} %get-tuple-element.15.LI, bf16[4,8,2,64,512]{4,3,2,1,0:T(8,128)(2,1)S(1)} %get-tuple-element.16.QD, bf16[128,2,64,128]{3,2,1,0:T(8,128)(2,1)S(1)} %bitcast.12, f32[4,8,8,128]{3,2,1,0:T(8,128)S(1)} %get-tuple-element.18.DL, ...), custom_call_target="tpu_custom_call" | custom-call | tf_op jit(solution)/shard_map/pair_grads/pallas_call | solution.py:488
  79.5 40.8 %reduce_rings.1 = (bf16[64,4096]{1,0:T(8,128)(2,1)S(1)}, bf16[64,1024]{1,0:T(8,128)(2,1)S(1)}, bf16[64,1024]{1,0:T(8,128)(2,1)S(1)}) custom-call(f32[4,8,64,512]{3,2,1,0:T(8,128)S(1)} %get-tuple-element.22.dq, f32[2,8,8,2,64,128]{5,4,3,2,1,0:T(8,128)S(1)} %bitcast.11), custom_call_target="tpu_custom_call" | custom-call | tf_op jit(solution)/shard_map/reduce_rings/pallas_call | solution.py:725
  120.3 0.9 finish.1
  (3 shorter events, 0.0 us)
Async XLA Ops:
  0.6 0.8 copy-start
